TPU v7x, 256 devices: a whole 4x4x8 slice. The times are simulated.
256 devices in a mesh: leaf: 64 (over z, y, core), head: 4 (over x).
Axes of the slice: x: 4, y: 4, z: 8, core: 2. Of those that a mesh axis runs over, the one named last changes fastest.
Arguments:
- queries: bfloat16 [32768, 4096], P('leaf', 'head'), may hold values from -180 to 180
- new_kv: bfloat16 [32768, 1024], P('leaf', 'head'), may hold values from -6 to 6
- prompt_kv: bfloat16 [1024, 1024], P('leaf', 'head'), may hold values from -6 to 6
- pool: bfloat16 [2048, 128, 1024], P('leaf', None, 'head'), may hold values from -6 to 6
- parents: int32 [256, 24], P('leaf'), may hold values from 0 to 2047, as said below
- lengths: int32 [256], P('leaf'), may hold values from 6 to 24, as said below
- location: int32 [2048], replicated, may hold values from 0 to 2047, as said below
- out_weight: bfloat16 [4096, 4096], P('head'), may hold values from -0.09375 to 0.09375
Outputs:
- mixed: bfloat16 [32768, 4096], P(('leaf', 'head'))
Inputs may be any that keep to these rules, and one draw needn't show every extreme that they name: `parents`: segment numbers of stored segments; the ancestors of one segment are distinct. `parents`: the live slots of the segments of one index of leaf name at most 2 slots stored on any one index of leaf; this bound is reached in every draw. `lengths`: every draw has a segment with 24 live ancestors. Each storage row once; segment b is stored on index location[b] // 32 of leaf.
All inputs are finite; a program needn't handle non-finite values.
Results may differ from a plain program's by a relative error of at most 0.018.
Values may be sent and summed in bfloat16 or wider, within the bound.
No kernel may reach another device: no remote copies, remote signals or barrier semaphores. Data moves between devices by JAX's collectives and lax.ppermute only.
A program may use at most 128 MiB of HBM per device.

v0:
```python
import jax
import jax.numpy as jnp
from jax import lax
from jax.sharding import PartitionSpec as P


def absorb(carry, scores, visible, product):
    running, total, summed = carry
    masked = jnp.where(visible, scores, jnp.float32(-1e30))
    newest = jnp.maximum(running, jnp.max(masked, axis=-1))
    factor = jnp.exp(running - newest)
    probs = jnp.where(visible, jnp.exp(masked - newest[..., None]), jnp.float32(0.0))
    total = total * factor + jnp.sum(probs, axis=-1)
    summed = summed * factor[..., None] + product(probs.astype(jnp.bfloat16))
    return (newest, total, summed)


def request_ranks(owner, chosen):
    count = owner.shape[0]
    order = jnp.arange(count)
    same = owner[:, None] == owner[None, :]
    earlier = order[:, None] > order[None, :]
    return jnp.sum(same & earlier & chosen[None, :], axis=1)


def per_device(queries, new_kv, prompt_kv, pool, parents, lengths, location, out_weight):
    tok_rows = queries.shape[0]
    seg_dev = parents.shape[0]
    max_anc = parents.shape[1]
    head_dim = prompt_kv.shape[1] // 2
    group = queries.shape[1] // head_dim
    seg_len = tok_rows // seg_dev
    blocks = pool.shape[0]
    scale = head_dim ** (-0.5)
    query = queries.reshape(tok_rows, group, head_dim)
    init = (
        jnp.full((group, tok_rows), -1e30, jnp.float32),
        jnp.zeros((group, tok_rows), jnp.float32),
        jnp.zeros((group, tok_rows, head_dim), jnp.float32),
    )
    piece = lax.all_gather(prompt_kv, "leaf", axis=0, tiled=True)
    scores = (
        jnp.einsum("tgd,nd->gtn", query, piece[:, :head_dim], preferred_element_type=jnp.float32)
        * scale
    )
    visible = jnp.ones(scores.shape, bool)

    def product(weights):
        return jnp.einsum(
            "gtn,nd->gtd", weights, piece[:, head_dim:], preferred_element_type=jnp.float32
        )

    running, total, summed = absorb(init, scores, visible, product)
    n_leaf = lax.axis_size("leaf")
    capacity = max(2, -(-(seg_dev * max_anc) // n_leaf))
    stored = location[parents].reshape(-1)
    live = (jnp.arange(max_anc)[None, :] < lengths[:, None]).reshape(-1)
    owner = stored // blocks
    local_row = stored % blocks
    ranks = request_ranks(owner, live)
    senders = jnp.where(live, owner, n_leaf)
    wanted = (
        jnp.full((n_leaf, capacity), -1, jnp.int32).at[senders, ranks].set(local_row, mode="drop")
    )
    picked = pool[
        jnp.clip(
            lax.all_to_all(wanted, "leaf", split_axis=0, concat_axis=0, tiled=True), 0, blocks - 1
        )
    ]
    arrived = lax.all_to_all(picked, "leaf", split_axis=0, concat_axis=0, tiled=True)
    fetched = arrived[owner, jnp.clip(ranks, 0, capacity - 1)].reshape(
        seg_dev, max_anc, seg_len, 2 * head_dim
    )
    segq = query.reshape(seg_dev, seg_len, group, head_dim)
    carry = (
        running.reshape(group, seg_dev, seg_len),
        total.reshape(group, seg_dev, seg_len),
        summed.reshape(group, seg_dev, seg_len, head_dim),
    )
    flat = fetched.reshape(seg_dev, max_anc * seg_len, 2 * head_dim)
    slot_of = jnp.arange(max_anc * seg_len) // seg_len

    def per_segment(items):
        seg_query, seg_keys, seg_live, seg_run, seg_total, seg_summed = items
        scores = (
            jnp.einsum(
                "qgd,kd->gqk", seg_query, seg_keys[:, :head_dim], preferred_element_type=jnp.float32
            )
            * scale
        )
        visible = jnp.broadcast_to((slot_of < seg_live)[None, None, :], scores.shape)

        def product(weights):
            return jnp.einsum(
                "gqk,kd->gqd", weights, seg_keys[:, head_dim:], preferred_element_type=jnp.float32
            )

        return absorb((seg_run, seg_total, seg_summed), scores, visible, product)

    result = lax.map(
        per_segment,
        (
            segq,
            flat,
            lengths,
            jnp.transpose(carry[0], (1, 0, 2)),
            jnp.transpose(carry[1], (1, 0, 2)),
            jnp.transpose(carry[2], (1, 0, 2, 3)),
        ),
    )
    carry = (
        jnp.transpose(result[0], (1, 0, 2)),
        jnp.transpose(result[1], (1, 0, 2)),
        jnp.transpose(result[2], (1, 0, 2, 3)),
    )
    own = new_kv.reshape(seg_dev, seg_len, 2 * head_dim)
    scores = (
        jnp.einsum("sqgd,skd->gsqk", segq, own[:, :, :head_dim], preferred_element_type=jnp.float32)
        * scale
    )
    causal = jnp.arange(seg_len)[:, None] >= jnp.arange(seg_len)[None, :]
    visible = jnp.broadcast_to(causal[None, None], scores.shape)

    def product_own(weights):
        return jnp.einsum(
            "gsqk,skd->gsqd", weights, own[:, :, head_dim:], preferred_element_type=jnp.float32
        )

    running, total, summed = absorb(carry, scores, visible, product_own)
    attended = (summed / total[..., None]).astype(jnp.bfloat16)
    attended = jnp.transpose(attended, (1, 2, 0, 3)).reshape(tok_rows, group * head_dim)
    return lax.psum_scatter(
        jnp.dot(attended, out_weight, preferred_element_type=jnp.float32).astype(jnp.bfloat16),
        "head",
        scatter_dimension=0,
        tiled=True,
    )


def solution(mesh):
    return jax.shard_map(
        per_device,
        mesh=mesh,
        in_specs=(
            P("leaf", "head"),
            P("leaf", "head"),
            P("leaf", "head"),
            P("leaf", None, "head"),
            P("leaf", None),
            P("leaf"),
            P(),
            P("head", None),
        ),
        out_specs=P(("leaf", "head"), None),
        check_vma=False,
    )
```

profile of v0, /device:TPU:6, one launch (start us, length us, event | category | flops | bytes accessed | tf_op | source)
XLA Modules:
  0.0 435.9 jit_solution(1901048192132077787)
XLA Ops:
  10.2 5.0 %scatter_fusion = s32[64,2]{0,1:T(2,128)S(1)} fusion(s32[64,2]{0,1:T(2,128)S(1)} %broadcast_in_dim.87, s32[96]{0:T(128)S(1)} %get-tuple-element.161, s32[96]{0:T(128)S(1)} %get-tuple-element.162), kind=kCustom, calls=%fused_computation.3 | custom fusion | bytes 1920 | tf_op jit(solution)/shard_map/scatter | solution.py:63
  15.3 21.5 %all_to_all.14 = s32[64,1,2]{2,1,0:T(1,128)S(1)} all-to-all(s32[64,1,2]{2,1,0:T(1,128)S(1)} %copy.48), channel_id=1, replica_groups=mesh['leaf'=64,'head'=4] {'leaf'}, dimensions={0} | all-to-all | bytes 1024 | tf_op jit(solution)/shard_map/all_to_all | solution.py:67
  37.2 6.5 %gather_fusion.1 = bf16[128,128,256]{2,1,0:T(8,128)(2,1)} fusion(bf16[32,128,256]{2,1,0:T(8,128)(2,1)S(1)} %copy-done, s32[1024]{0:T(1024)S(1)} %pad_clamp_fusion), kind=kCustom, calls=%fused_computation.1 | custom fusion | bytes 16777728 | tf_op jit(solution)/shard_map/gather | solution.py:65
  43.7 5.9 %all-to-all-start.1 = ((bf16[64,2,128,256]{3,2,1,0:T(8,128)(2,1)}), bf16[64,2,128,256]{3,2,1,0:T(8,128)(2,1)}, u32[]{:S(2)}, u32[]{:S(2)}) async-start(bf16[64,2,128,256]{3,2,1,0:T(8,128)(2,1)} %bitcast.225), calls=%async_computation.1 | async-start | bytes 16777216 | tf_op jit(solution)/shard_map/all_to_all | solution.py:70
  50.2 226.2 %all_gather.3 = bf16[1024,256]{1,0:T(8,128)(2,1)S(1)} all-gather(bf16[16,256]{1,0:T(8,128)(2,1)S(1)} %copy-done.5), channel_id=1, replica_groups=mesh['leaf'=64,'head'=4] {'leaf'}, dimensions={0}, use_global_device_ids=true | all-gather | bytes 532480 | tf_op jit(solution)/shard_map/all_gather | solution.py:41
  276.3 2.4 bitcast_reduce_fusion.1
  278.7 3.6 fusion.43
  282.4 2.0 copy-done.2
  285.9 8.5 %fusion.35 = f32[8,512]{1,0:T(8,128)S(1)} fusion(f32[1024,512,8]{1,0,2:T(8,128)} %copy-done.2, f32[8,512]{1,0:T(8,128)S(1)} %get-tuple-element.159), kind=kLoop, calls=%fused_computation.48 | loop fusion | flops 12578816 | bytes 16809984 | tf_op jit(solution)/shard_map/reduce_sum | solution.py:13
  296.3 10.2 %gather_fusion.2 = bf16[96,128,256]{2,1,0:T(8,128)(2,1)} fusion(bf16[64,2,128,256]{3,2,1,0:T(8,128)(2,1)} %all-to-all-done.1, s32[96]{0:T(128)S(1)} %get-tuple-element.160), kind=kCustom, calls=%fused_computation.2 | custom fusion | bytes 12583680 | tf_op jit(solution)/shard_map/gather | solution.py:71
  306.6 60.2 %while.15 = (s32[]{:T(128)}, f32[4,8,128]{2,1,0:T(8,128)S(1)}, f32[4,8,128]{2,1,0:T(8,128)S(1)}, f32[4,8,128,128]{3,2,1,0:T(8,128)}, f32[4,8,128]{2,1,0:T(8,128)...) while((s32[]{:T(128)}, f32[4,8,128]{2,1,0:T(8,128)S(1)}, ...), condition=%wide.region_7.8_spmd.clone, body=%wide.region_4.7_spmd.clone.sunk | while | flops 1651801088 | bytes 43855000 | solution.py:100
  311.2 4.1 fusion.92
  315.3 6.3 %fusion.94 = f32[4,8,128,128]{3,2,1,0:T(8,128)} fusion(f32[4,8,128,128]{3,2,1,0:T(8,128)} %get-tuple-element.255, s32[]{:T(128)S(6)} %copy.89, f32[3072,128,8]{1,0,2:T(8,128)S(1)} %get-tuple-element.235, f32[8,128]{1,0:T(8,128)S(1)} %get-tuple-element.237, pred[3072]{0:T(1024)(128)(4,1)S(1)} %fusion.90, ...), kind=kOutput, calls=%fused_computation.18.clone.1 | convolution fusion | flops 821297152 | bytes 14432260 | tf_op jit(solution)/shard_map/while/body/eval_jaxpr/gqk,kd->gqd/dot_general | solution.py:94
  326.2 4.1 fusion.92
  330.4 6.3 %fusion.94 = f32[4,8,128,128]{3,2,1,0:T(8,128)} fusion(f32[4,8,128,128]{3,2,1,0:T(8,128)} %get-tuple-element.255, s32[]{:T(128)S(6)} %copy.89, f32[3072,128,8]{1,0,2:T(8,128)S(1)} %get-tuple-element.235, f32[8,128]{1,0:T(8,128)S(1)} %get-tuple-element.237, pred[3072]{0:T(1024)(128)(4,1)S(1)} %fusion.90, ...), kind=kOutput, calls=%fused_computation.18.clone.1 | convolution fusion | flops 821297152 | bytes 14432260 | tf_op jit(solution)/shard_map/while/body/eval_jaxpr/gqk,kd->gqd/dot_general | solution.py:94
  341.3 4.1 fusion.92
  345.4 6.3 %fusion.94 = f32[4,8,128,128]{3,2,1,0:T(8,128)} fusion(f32[4,8,128,128]{3,2,1,0:T(8,128)} %get-tuple-element.255, s32[]{:T(128)S(6)} %copy.89, f32[3072,128,8]{1,0,2:T(8,128)S(1)} %get-tuple-element.235, f32[8,128]{1,0:T(8,128)S(1)} %get-tuple-element.237, pred[3072]{0:T(1024)(128)(4,1)S(1)} %fusion.90, ...), kind=kOutput, calls=%fused_computation.18.clone.1 | convolution fusion | flops 821297152 | bytes 14432260 | tf_op jit(solution)/shard_map/while/body/eval_jaxpr/gqk,kd->gqd/dot_general | solution.py:94
  354.4 1.9 bitcast_reduce_fusion.3
  356.3 4.1 fusion.92
  360.5 6.3 %fusion.94 = f32[4,8,128,128]{3,2,1,0:T(8,128)} fusion(f32[4,8,128,128]{3,2,1,0:T(8,128)} %get-tuple-element.255, s32[]{:T(128)S(6)} %copy.89, f32[3072,128,8]{1,0,2:T(8,128)S(1)} %get-tuple-element.235, f32[8,128]{1,0:T(8,128)S(1)} %get-tuple-element.237, pred[3072]{0:T(1024)(128)(4,1)S(1)} %fusion.90, ...), kind=kOutput, calls=%fused_computation.18.clone.1 | convolution fusion | flops 821297152 | bytes 14432260 | tf_op jit(solution)/shard_map/while/body/eval_jaxpr/gqk,kd->gqd/dot_general | solution.py:94
  366.8 2.1 fusion.46
  368.9 3.4 fusion.41
  373.0 9.5 %convolution_convert_fusion = bf16[512,4096]{1,0:T(8,128)(2,1)} fusion(bf16[1024,4096]{1,0:T(8,128)(2,1)} %param.17, bf16[64,8,8,128]{3,2,1,0:T(8,128)(2,1)S(1)} %bitcast.232), kind=kOutput, calls=%fused_computation.52 | convolution fusion | flops 4297064448 | bytes 13631488 | tf_op jit(solution)/shard_map/dot_general | solution.py:133
  382.6 46.5 %reduce-scatter.2.cloned.1.call-done = bf16[128,4096]{1,0:T(8,128)(2,1)} async-done(((bf16[512,4096]{1,0:T(8,128)(2,1)}), bf16[128,4096]{1,0:T(8,128)(2,1)}) %reduce-scatter.2.cloned.1.call-update) | async-done | bytes 1048592 | tf_op jit(solution)/shard_map/reduce_scatter | solution.py:132
  (69 shorter events, 25.2 us)
Async XLA Ops:
  6.5 30.6 %copy-start = (bf16[32,128,256]{2,1,0:T(8,128)(2,1)S(1)}, bf16[32,128,256]{2,1,0:T(8,128)(2,1)}, u32[]{:S(2)}) copy-start(bf16[32,128,256]{2,1,0:T(8,128)(2,1)} %param.13) | copy-start | bytes 6291460
  43.7 6.0 %copy-start.3 = (bf16[512,1024]{1,0:T(8,128)(2,1)S(1)}, bf16[512,1024]{1,0:T(8,128)(2,1)}, u32[]{:S(2)}) copy-start(bf16[512,1024]{1,0:T(8,128)(2,1)} %param.10) | copy-start | bytes 3145732
  43.7 6.5 %copy-start.5 = (bf16[16,256]{1,0:T(8,128)(2,1)S(1)}, bf16[16,256]{1,0:T(8,128)(2,1)}, u32[]{:S(2)}) copy-start(bf16[16,256]{1,0:T(8,128)(2,1)} %param.12) | copy-start | bytes 24580
  43.7 252.6 %all-to-all-start.1 = ((bf16[64,2,128,256]{3,2,1,0:T(8,128)(2,1)}), bf16[64,2,128,256]{3,2,1,0:T(8,128)(2,1)}, u32[]{:S(2)}, u32[]{:S(2)}) async-start(bf16[64,2,128,256]{3,2,1,0:T(8,128)(2,1)} %bitcast.225), calls=%async_computation.1 | async-start | bytes 16777216 | tf_op jit(solution)/shard_map/all_to_all | solution.py:70
  49.6 379.5 %reduce-scatter.2.cloned.1.call-start = ((), (), s32[]{:S(2)}) async-start(), calls=%async_computation.3 | async-start | bytes 5242880 | tf_op jit(solution)/shard_map/reduce_scatter | solution.py:132
  278.7 5.7 %copy-start.2 = (f32[1024,512,8]{1,0,2:T(8,128)}, f32[1024,512,8]{1,0,2:T(8,128)S(1)}, u32[]{:S(2)}) copy-start(f32[1024,512,8]{1,0,2:T(8,128)S(1)} %get-tuple-element.165) | copy-start | bytes 50331652
  285.9 8.6 %copy-start.4 = (bf16[512,256]{1,0:T(8,128)(2,1)S(1)}, bf16[512,256]{1,0:T(8,128)(2,1)}, u32[]{:S(2)}) copy-start(bf16[512,256]{1,0:T(8,128)(2,1)} %param.11) | copy-start | bytes 786436
  296.3 10.3 %copy-start.6 = (s32[4]{0:T(128)S(1)}, s32[4]{0:T(128)}, u32[]{:S(2)}) copy-start(s32[4]{0:T(128)} %param.15) | copy-start | bytes 52
  373.0 56.0 %copy-start.1 = (bf16[32,128,256]{2,1,0:T(8,128)(2,1)S(1)}, bf16[32,128,256]{2,1,0:T(8,128)(2,1)}, u32[]{:S(2)}) copy-start(bf16[32,128,256]{2,1,0:T(8,128)(2,1)} %param.13) | copy-start | bytes 6291460
Sparse Core Ops, SparseCore 0:
  382.7 46.2 reduce-scatter.1
where the time goes:
time: 439 us; the launch traced here: 436 us
  blocking collectives  248 us (56%)
  matrix products  53.6 us (12%)
  waiting for transfers between devices  46.5 us (11%)
  local copies, waits for them, and re-layouts  37.1 us (8%)
  other arithmetic  31.4 us (7%)
  between operations  13.6 us (3%)
  starting transfers between devices  5.92 us (1%)
    all_gather x1, blocking collectives, per_device(): piece = lax.all_gather(prompt_kv, 'leaf', axis=0, tiled=True)  226 us
    reduce_scatter x1, waiting for transfers between devices, per_device(): lax.psum_scatter(jnp.dot(attended, out_weight, preferred_element_type=jnp...  46.5 us
    reduce_sum x6, other arithmetic, absorb(): total = total * factor + jnp.sum(probs, axis=-1)  27.2 us
    dot_general x4, matrix products, product(): jnp.einsum('gqk,kd->gqd', weights, seg_keys[:, head_dim:], preferred_elem...  25.2 us
    all_to_all x1, blocking collectives, per_device(): lax.all_to_all(wanted, 'leaf', split_axis=0, concat_axis=0, tiled=True)  21.5 us
    gather x1, local copies, waits for them, and re-layouts, per_device(): arrived[owner, jnp.clip(ranks, 0, capacity - 1)]  10.2 us
    dot_general x1, matrix products, per_device(): jnp.dot(attended, out_weight, preferred_element_type=jnp.float32)  9.54 us
  transfers between devices with their start and end apart: 2, of which 1 were waited for; matrix products, arithmetic and copies ran while one was open for 4% of the time, Pallas kernels for 0%

commit v1 on v0

v1 whole, which is shorter than its diff:
```python
import functools

import jax
import jax.numpy as jnp
from jax import lax
from jax.experimental import pallas as pl
from jax.experimental.pallas import tpu as pltpu
from jax.sharding import PartitionSpec as P

Y_SIZE = 4
CORES = 2
LANES = Y_SIZE * CORES
LOG2E = 1.4426950408889634
TILE = 256


def absorb(seg, keys, values, q_ref, m_ref, l_ref, acc_ref, scale, mask=None, first=False):
    factor = scale * LOG2E
    for at in range(0, q_ref.shape[2], TILE):
        cols = slice(at, at + TILE)
        scores = jnp.dot(keys, q_ref[seg, :, cols], preferred_element_type=jnp.float32)
        if mask is not None:
            scores = jnp.where(mask, scores, jnp.float32(-1e30))
        top = jnp.max(scores, axis=0, keepdims=True)
        if not first:
            before = m_ref[seg, :, cols]
            top = jnp.maximum(before, top)
        probs = jnp.exp2((scores - top) * factor)
        total = jnp.sum(probs, axis=0, keepdims=True)
        summed = lax.dot_general(
            values,
            probs.astype(jnp.bfloat16),
            (((0,), (0,)), ((), ())),
            preferred_element_type=jnp.float32,
        )
        if not first:
            shrink = jnp.exp2((before - top) * factor)
            total = total + l_ref[seg, :, cols] * shrink
            summed = summed + acc_ref[seg, :, cols] * shrink
        m_ref[seg, :, cols] = top
        l_ref[seg, :, cols] = total
        acc_ref[seg, :, cols] = summed


def absorb_blocks(seg_ref, blocks_ref, q_ref, m_ref, l_ref, acc_ref, list_ref, count_ref, scale):
    places = seg_ref.shape[0]
    segs = q_ref.shape[0]
    head_dim = q_ref.shape[1]
    for seg in range(segs):
        count_ref[seg] = 0

    def place(at, carry):
        seg = seg_ref[at]

        @pl.when(seg >= 0)
        def _():
            used = count_ref[seg]
            list_ref[seg * places + used] = at
            count_ref[seg] = used + 1

        return carry

    lax.fori_loop(0, places, place, 0)

    def per_segment(seg, carry):
        count = count_ref[seg]

        def pair(step, inner):
            one = list_ref[seg * places + 2 * step]
            two = list_ref[seg * places + 2 * step + 1]
            keys = jnp.concatenate(
                [blocks_ref[one, :, :head_dim], blocks_ref[two, :, :head_dim]], axis=0
            )
            values = jnp.concatenate(
                [blocks_ref[one, :, head_dim:], blocks_ref[two, :, head_dim:]], axis=0
            )
            absorb(seg, keys, values, q_ref, m_ref, l_ref, acc_ref, scale)
            return inner

        lax.fori_loop(0, count // 2, pair, 0)

        @pl.when(count % 2 == 1)
        def _():
            last = list_ref[seg * places + count - 1]
            absorb(
                seg,
                blocks_ref[last, :, :head_dim],
                blocks_ref[last, :, head_dim:],
                q_ref,
                m_ref,
                l_ref,
                acc_ref,
                scale,
            )

        return carry

    lax.fori_loop(0, segs, per_segment, 0)


def first_kernel(scale, seg_ref, q_ref, own_ref, blocks_ref, m_ref, l_ref, acc_ref, list_ref, count_ref):
    head_dim = q_ref.shape[1]
    seg_len = own_ref.shape[1]
    key_at = lax.broadcasted_iota(jnp.int32, (seg_len, TILE), 0)
    query_at = lax.broadcasted_iota(jnp.int32, (seg_len, TILE), 1) % seg_len
    causal = query_at >= key_at

    def own(seg, carry):
        absorb(
            seg,
            own_ref[seg, :, :head_dim],
            own_ref[seg, :, head_dim:],
            q_ref,
            m_ref,
            l_ref,
            acc_ref,
            scale,
            mask=causal,
            first=True,
        )
        return carry

    lax.fori_loop(0, q_ref.shape[0], own, 0)
    absorb_blocks(seg_ref, blocks_ref, q_ref, m_ref, l_ref, acc_ref, list_ref, count_ref, scale)


def carry_in(old, new):
    for source, target in zip(old, new):
        target[...] = source[...]


def prompt_kernel(scale, q_ref, prompt_ref, m_in, l_in, acc_in, m_ref, l_ref, acc_ref):
    head_dim = q_ref.shape[1]
    carry_in((m_in, l_in, acc_in), (m_ref, l_ref, acc_ref))

    def step(at, carry):
        seg = at % q_ref.shape[0]
        rows = pl.ds(pl.multiple_of((at // q_ref.shape[0]) * TILE, TILE), TILE)
        absorb(
            seg,
            prompt_ref[rows, :head_dim],
            prompt_ref[rows, head_dim:],
            q_ref,
            m_ref,
            l_ref,
            acc_ref,
            scale,
        )
        return carry

    lax.fori_loop(0, q_ref.shape[0] * (prompt_ref.shape[0] // TILE), step, 0)


def chunk_kernel(scale, seg_ref, q_ref, blocks_ref, m_in, l_in, acc_in, m_ref, l_ref, acc_ref, list_ref, count_ref):
    carry_in((m_in, l_in, acc_in), (m_ref, l_ref, acc_ref))
    absorb_blocks(seg_ref, blocks_ref, q_ref, m_ref, l_ref, acc_ref, list_ref, count_ref, scale)


def last_kernel(scale, seg_ref, q_ref, blocks_ref, m_in, l_in, acc_in, out_ref, m_ref, l_ref, acc_ref, list_ref, count_ref):
    carry_in((m_in, l_in, acc_in), (m_ref, l_ref, acc_ref))
    absorb_blocks(seg_ref, blocks_ref, q_ref, m_ref, l_ref, acc_ref, list_ref, count_ref, scale)
    seg_len = out_ref.shape[1]
    head_dim = q_ref.shape[1]
    group = q_ref.shape[2] // seg_len

    def finish(seg, carry):
        for g in range(group):
            cols = slice(g * seg_len, (g + 1) * seg_len)
            value = acc_ref[seg, :, cols] / l_ref[seg, :, cols]
            out_ref[seg, :, g * head_dim : (g + 1) * head_dim] = value.T.astype(jnp.bfloat16)
        return carry

    lax.fori_loop(0, q_ref.shape[0], finish, 0)


VMEM = pl.BlockSpec(memory_space=pltpu.VMEM)
SMEM = pl.BlockSpec(memory_space=pltpu.SMEM)


def state_shapes(q):
    segs, head_dim, columns = q.shape
    return [
        jax.ShapeDtypeStruct((segs, 1, columns), jnp.float32),
        jax.ShapeDtypeStruct((segs, 1, columns), jnp.float32),
        jax.ShapeDtypeStruct((segs, head_dim, columns), jnp.float32),
    ]


def cost(q, blocks):
    work = blocks * 128 * q.shape[2] * q.shape[1]
    return pl.CostEstimate(flops=8 * work, bytes_accessed=6 * q.size, transcendentals=work // 128)


def params():
    return pltpu.CompilerParams(vmem_limit_bytes=40 * 1024 * 1024)


def tables(places, segs):
    return [pltpu.SMEM((segs * places,), jnp.int32), pltpu.SMEM((segs,), jnp.int32)]


def attend_first(q, own, seg_of, blocks, scale):
    return pl.pallas_call(
        functools.partial(first_kernel, scale),
        out_shape=state_shapes(q),
        in_specs=[SMEM, VMEM, VMEM, VMEM],
        out_specs=[VMEM] * 3,
        scratch_shapes=tables(seg_of.shape[0], q.shape[0]),
        compiler_params=params(),
        cost_estimate=cost(q, 12),
    )(seg_of, q, own, blocks)


def attend_prompt(q, prompt, state, scale):
    return pl.pallas_call(
        functools.partial(prompt_kernel, scale),
        out_shape=state_shapes(q),
        in_specs=[VMEM] * 5,
        out_specs=[VMEM] * 3,
        compiler_params=params(),
        cost_estimate=cost(q, 32),
    )(q, prompt, *state)


def attend_chunk(q, seg_of, blocks, state, scale):
    return pl.pallas_call(
        functools.partial(chunk_kernel, scale),
        out_shape=state_shapes(q),
        in_specs=[SMEM] + [VMEM] * 5,
        out_specs=[VMEM] * 3,
        scratch_shapes=tables(seg_of.shape[0], q.shape[0]),
        compiler_params=params(),
        cost_estimate=cost(q, 16),
    )(seg_of, q, blocks, *state)


def attend_last(q, seg_of, blocks, state, scale):
    segs, head_dim, columns = q.shape
    seg_len = blocks.shape[1]
    group = columns // seg_len
    return pl.pallas_call(
        functools.partial(last_kernel, scale),
        out_shape=jax.ShapeDtypeStruct((segs, seg_len, group * head_dim), jnp.bfloat16),
        in_specs=[SMEM] + [VMEM] * 5,
        out_specs=VMEM,
        scratch_shapes=[pltpu.VMEM(s.shape, s.dtype) for s in state_shapes(q)]
        + tables(seg_of.shape[0], segs),
        compiler_params=params(),
        cost_estimate=cost(q, 8),
    )(seg_of, q, blocks, *state)


def per_device(queries, new_kv, prompt_kv, pool, parents, lengths, location, out_weight):
    tok_rows = queries.shape[0]
    seg_dev, max_anc = parents.shape
    head_dim = prompt_kv.shape[1] // 2
    group = queries.shape[1] // head_dim
    seg_len = tok_rows // seg_dev
    blocks = pool.shape[0]
    scale = head_dim ** (-0.5)
    n_leaf = lax.axis_size("leaf")
    planes = n_leaf // LANES
    capacity = 2
    me = lax.axis_index("leaf")
    plane = me // LANES

    def along_z(x, step):
        pairs = [(d, (d + step * LANES) % n_leaf) for d in range(n_leaf)]
        return lax.ppermute(x, "leaf", pairs)

    in_plane = [[p * LANES + lane for lane in range(LANES)] for p in range(planes)]

    def spread(x):
        return lax.all_to_all(x, "leaf", 0, 0, tiled=True, axis_index_groups=in_plane)

    up1 = along_z(pool, 1)
    down1 = along_z(pool, -1)

    prompt = lax.all_gather(prompt_kv, "leaf", axis=0, tiled=True)

    slots = seg_dev * max_anc
    stored = location[parents].reshape(-1)
    live = (jnp.arange(max_anc)[None, :] < lengths[:, None]).reshape(-1)
    owner = jnp.where(live, stored // blocks, -1)
    row = stored % blocks
    order = jnp.arange(slots)
    rank = jnp.sum(
        (owner[:, None] == owner[None, :]) & (order[:, None] > order[None, :]), axis=1
    )
    dist = (plane - owner // LANES) % planes
    cell = jnp.where(live, (dist * LANES + owner % LANES) * capacity + rank, -1)
    hit = cell[None, :] == jnp.arange(n_leaf * capacity)[:, None]
    wanted = jnp.sum(jnp.where(hit, row[None, :], 0), axis=1).astype(jnp.int32)
    seg_of = jnp.sum(jnp.where(hit, (order // max_anc + 1)[None, :], 0), axis=1) - 1
    seg_of = seg_of.astype(jnp.int32).reshape(planes, LANES, capacity)
    per_lane = jnp.transpose(wanted.reshape(planes, LANES, capacity), (1, 0, 2))
    ask = jnp.broadcast_to(
        per_lane.reshape(1, LANES, 1, planes * capacity), (planes, LANES, 1, planes * capacity)
    ).reshape(n_leaf, 1, planes * capacity)
    asked = lax.all_to_all(ask, "leaf", split_axis=0, concat_axis=0, tiled=True)
    asked = asked.reshape(planes, LANES, planes, capacity)
    asked = lax.dynamic_slice_in_dim(jnp.concatenate([asked, asked], axis=0), plane, planes, 0)
    here = asked[0]

    def pick(buffer, rows):
        return buffer[rows.reshape(-1)].reshape(rows.shape + buffer.shape[1:])

    def segs_at(dists):
        return jnp.stack([seg_of[d] for d in dists], axis=1).reshape(-1)

    def flat(x):
        return x.reshape((-1,) + x.shape[-2:])

    q = jnp.transpose(
        queries.reshape(seg_dev, seg_len, group, head_dim), (0, 3, 2, 1)
    ).reshape(seg_dev, head_dim, group * seg_len)
    own = new_kv.reshape(seg_dev, seg_len, 2 * head_dim)

    got0 = spread(pick(pool, here[:, 0]))
    state = attend_first(q, own, segs_at([0]), flat(got0), scale)

    up2 = along_z(up1, 1)
    down2 = along_z(down1, -1)
    got1 = spread(jnp.stack([pick(up1, here[:, 1]), pick(down1, here[:, planes - 1])], axis=1))
    state = attend_chunk(q, segs_at([1, planes - 1]), flat(got1), state, scale)

    state = attend_prompt(q, prompt, state, scale)

    half = LANES // 2
    far_up = pick(up2, asked[2, :half, 4])
    far_down = pick(down2, asked[planes - 2, half:, 4])
    near_up = pick(up2, asked[1, :, 3])
    near_down = pick(down2, asked[planes - 1, :, planes - 3])
    far_up3 = along_z(far_up, 1)
    far_down3 = along_z(far_down, -1)
    up3 = along_z(near_up, 1)
    down3 = along_z(near_down, -1)
    got2 = spread(jnp.stack([pick(up2, here[:, 2]), pick(down2, here[:, planes - 2])], axis=1))
    far_up4 = along_z(far_up3, 1)
    far_down4 = along_z(far_down3, -1)
    state = attend_chunk(q, segs_at([2, planes - 2]), flat(got2), state, scale)

    got3 = spread(jnp.stack([up3, down3], axis=1))
    state = attend_chunk(q, segs_at([3, planes - 3]), flat(got3), state, scale)

    got4 = spread(jnp.concatenate([far_up4, far_down4], axis=0))
    attended = attend_last(q, segs_at([4]), flat(got4), state, scale)

    return lax.psum_scatter(
        jnp.dot(
            attended.reshape(tok_rows, group * head_dim),
            out_weight,
            preferred_element_type=jnp.float32,
        ).astype(jnp.bfloat16),
        "head",
        scatter_dimension=0,
        tiled=True,
    )


def solution(mesh):
    return jax.shard_map(
        per_device,
        mesh=mesh,
        in_specs=(
            P("leaf", "head"),
            P("leaf", "head"),
            P("leaf", "head"),
            P("leaf", None, "head"),
            P("leaf", None),
            P("leaf"),
            P(),
            P("head", None),
        ),
        out_specs=P(("leaf", "head"), None),
        check_vma=False,
    )
```

time: 439 us -> 420 us (0.957)
  blocking collectives: 248 us -> 54.4 us
  waiting for transfers between devices: 46.5 us -> 148 us
  Pallas kernels: 0 us -> 89 us
  matrix products: 53.6 us -> 9.48 us
  starting transfers between devices: 5.92 us -> 48.9 us
  other arithmetic: 31.4 us -> 11.3 us
    all_gather x1, blocking collectives: 226 us -> 54.4 us  [per_device(): prompt = lax.all_gather(prompt_kv, 'leaf', axis=0, tiled=True)]
    pallas_call x0 -> x6, Pallas kernels: none -> 89 us  [the longest x3 53.4 us: attend_chunk(): pl.pallas_call(functools.partial(chunk_kernel, scale), out_shape=state_sh...]
    ppermute x0 -> x10, waiting for transfers between devices: none -> 63.5 us  [along_z(): return lax.ppermute(x, 'leaf', pairs)]
    dot_general x13 -> x1, matrix products: 53.6 us -> 9.48 us  [per_device(): jnp.dot(attended.reshape(tok_rows, group * head_dim), out_weight, preferr...]
    all_to_all x1 -> x6, waiting for transfers between devices: 0.01 us -> 43.4 us  [the longest x1 37.3 us: per_device(): asked = lax.all_to_all(ask, 'leaf', split_axis=0, concat_axis=0, tiled=True)]
    reduce_sum x7 -> x2, other arithmetic: 27.4 us -> 0.29 us  [the longest x1 0.17 us: per_device(): jnp.sum((owner[:, None] == owner[None, :]) & (order[:, None] > order[None...]
    all_to_all x1 -> x6, starting transfers between devices: 5.88 us -> 29.1 us  [the longest x5 19.6 us: spread(): lax.all_to_all(x, 'leaf', 0, 0, tiled=True, axis_index_groups=in_plane)]
    all_to_all x1 -> x0, blocking collectives: 21.5 us -> none  [per_device(): lax.all_to_all(wanted, 'leaf', split_axis=0, concat_axis=0, tiled=True)]
  transfers between devices with their start and end apart: 2 -> 17, of which waited for: 1 -> 8; matrix products, arithmetic and copies ran while one was open for 4% -> 10% of each run, Pallas kernels for 0% -> 21%
where the time goes in v1:
time: 420 us; the launch traced here: 416 us
  waiting for transfers between devices  148 us (35%)
  Pallas kernels  89 us (21%)
  blocking collectives  54.4 us (13%)
  starting transfers between devices  48.9 us (12%)
  local copies, waits for them, and re-layouts  41.2 us (10%)
  between operations  13.9 us (3%)
  other arithmetic  11.3 us (3%)
  matrix products  9.48 us (2%)
    ppermute x10, waiting for transfers between devices, along_z(): return lax.ppermute(x, 'leaf', pairs)  63.5 us
    all_gather x1, blocking collectives, per_device(): prompt = lax.all_gather(prompt_kv, 'leaf', axis=0, tiled=True)  54.4 us
    pallas_call x3, Pallas kernels, attend_chunk(): pl.pallas_call(functools.partial(chunk_kernel, scale), out_shape=state_sh...  53.4 us
    reduce_scatter x1, waiting for transfers between devices, per_device(): lax.psum_scatter(jnp.dot(attended.reshape(tok_rows, group * head_dim), ou...  41.3 us
    all_to_all x1, waiting for transfers between devices, per_device(): asked = lax.all_to_all(ask, 'leaf', split_axis=0, concat_axis=0, tiled=True)  37.3 us
    gather x9, local copies, waits for them, and re-layouts, pick(): return buffer[rows.reshape(-1)].reshape(rows.shape + buffer.shape[1:])  20.1 us
    pallas_call x1, Pallas kernels, attend_prompt(): pl.pallas_call(functools.partial(prompt_kernel, scale), out_shape=state_s...  20 us
    ppermute x10, starting transfers between devices, along_z(): return lax.ppermute(x, 'leaf', pairs)  19.8 us
  transfers between devices with their start and end apart: 17, of which 8 were waited for; matrix products, arithmetic and copies ran while one was open for 10% of the time, Pallas kernels for 21%

profile of v1, /device:TPU:6, one launch (start us, length us, event | category | flops | bytes accessed | tf_op | source)
XLA Modules:
  0.0 416.4 jit_solution(11707889778228148121)
XLA Ops:
  8.5 3.9 collective-permute-start.4
  16.5 9.5 %all-to-all-start = ((s32[64,1,16]{2,1,0:T(1,128)}), s32[64,1,16]{2,1,0:T(1,128)S(1)}, u32[]{:S(2)}, u32[]{:S(2)}) async-start(s32[64,1,16]{2,1,0:T(1,128)} %bitcast.4), calls=%async_computation | async-start | bytes 65536 | tf_op jit(solution)/shard_map/all_to_all | solution.py:300
  26.0 37.3 %all-to-all-done = s32[64,1,16]{2,1,0:T(1,128)S(1)} async-done(((s32[64,1,16]{2,1,0:T(1,128)}), s32[64,1,16]{2,1,0:T(1,128)S(1)}, u32[]{:S(2)}, u32[]{:S(2)}) %all-to-all-start) | async-done | bytes 4128 | tf_op jit(solution)/shard_map/all_to_all | solution.py:300
  65.5 3.6 all-to-all-start.5
  78.8 6.1 %all-to-all-done.5 = bf16[8,2,128,256]{3,2,1,0:T(8,128)(2,1)S(1)} async-done(((bf16[8,2,128,256]{3,2,1,0:T(8,128)(2,1)}), bf16[8,2,128,256]{3,2,1,0:T(8,128)(2,1)S(1)}, u32[]{:S(2)}, u32[]{:S(2)}) %all-to-all-start.5) | async-done | bytes 1048608 | tf_op jit(solution)/shard_map/all_to_all | solution.py:274
  85.9 3.6 all-to-all-start.4
  90.3 28.7 %collective-permute-done.1 = bf16[32,128,256]{2,1,0:T(8,128)(2,1)} collective-permute-done((bf16[32,128,256]{2,1,0:T(8,128)(2,1)}, bf16[32,128,256]{2,1,0:T(8,128)(2,1)}, u32[]{:S(2)}, u32[]{:S(2)}) %collective-permute-start.1) | collective-permute-done | bytes 2097184 | tf_op jit(solution)/shard_map/ppermute | solution.py:269
  121.3 3.2 gather_fusion.6
  127.3 4.4 %all-to-all-start.3 = ((bf16[8,2,2,128,256]{4,3,2,1,0:T(8,128)(2,1)}), bf16[8,2,2,128,256]{4,3,2,1,0:T(8,128)(2,1)}, u32[]{:S(2)}, u32[]{:S(2)}) async-start(bf16[8,2,2,128,256]{4,3,2,1,0:T(8,128)(2,1)} %pad_maximum_fusion.1), calls=%async_computation.3 | async-start | bytes 4194304 | tf_op jit(solution)/shard_map/all_to_all | solution.py:274
  139.8 21.0 %collective-permute-done.8 = bf16[8,2,128,256]{3,2,1,0:T(8,128)(2,1)S(1)} collective-permute-done((bf16[8,2,128,256]{3,2,1,0:T(8,128)(2,1)S(1)}, bf16[8,2,128,256]{3,2,1,0:T(8,128)(2,1)S(1)}, u32[]{:S(2)}, u32[]{:S(2)}) %collective-permute-start.8) | collective-permute-done | bytes 1048608 | tf_op jit(solution)/shard_map/ppermute | solution.py:269
  163.2 2.8 pad_maximum_fusion
  166.0 4.4 %all-to-all-start.2 = ((bf16[8,2,2,128,256]{4,3,2,1,0:T(8,128)(2,1)}), bf16[8,2,2,128,256]{4,3,2,1,0:T(8,128)(2,1)S(1)}, u32[]{:S(2)}, u32[]{:S(2)}) async-start(bf16[8,2,2,128,256]{4,3,2,1,0:T(8,128)(2,1)} %pad_maximum_fusion), calls=%async_computation.2 | async-start | bytes 4194304 | tf_op jit(solution)/shard_map/all_to_all | solution.py:274
  178.7 9.9 %collective-permute-done.2 = bf16[4,2,128,256]{3,2,1,0:T(8,128)(2,1)} collective-permute-done((bf16[4,2,128,256]{3,2,1,0:T(8,128)(2,1)S(1)}, bf16[4,2,128,256]{3,2,1,0:T(8,128)(2,1)}, u32[]{:S(2)}, u32[]{:S(2)}) %collective-permute-start.2) | collective-permute-done | bytes 524320 | tf_op jit(solution)/shard_map/ppermute | solution.py:269
  190.0 3.8 collective-permute-start.7
  199.2 54.4 %all_gather.3.prompt_ref = bf16[1024,256]{1,0:T(8,128)(2,1)} all-gather(bf16[16,256]{1,0:T(8,128)(2,1)S(1)} %copy-done.15), channel_id=1, replica_groups=mesh['leaf'=64,'head'=4] {'leaf'}, dimensions={0}, use_global_device_ids=true | all-gather | bytes 532480 | tf_op jit(solution)/shard_map/all_gather | solution.py:279
  254.8 12.7 %shard_map.82 = (f32[4,1,1024]{2,1,0:T(1,128)S(1)}, f32[4,1,1024]{2,1,0:T(1,128)S(1)}, f32[4,128,1024]{2,1,0:T(8,128)S(1)}) custom-call(s32[16]{0:T(128)S(1)} %get-tuple-element.46.seg_ref, bf16[4,128,1024]{2,1,0:T(8,128)(2,1)S(1)} %reshape.544.q_ref, bf16[4,128,256]{2,1,0:T(8,128)(2,1)S(1)} %bitcast.87, bf16[16,128,256]{2,1,0:T(8,128)(2,1)S(1)} %bitcast.85), custom_call_target="tpu_custom_call" | custom-call | flops 1610612736 | bytes 3145728 | tf_op jit(solution)/shard_map/pallas_call | solution.py:203
  272.6 3.6 all-to-all-start.1
  279.4 21.1 %shard_map.83 = (f32[4,1,1024]{2,1,0:T(1,128)S(1)}, f32[4,1,1024]{2,1,0:T(1,128)S(1)}, f32[4,128,1024]{2,1,0:T(8,128)S(1)}) custom-call(s32[32]{0:T(128)S(1)} %reshape.556.seg_ref, bf16[4,128,1024]{2,1,0:T(8,128)(2,1)S(1)} %reshape.544.q_ref, bf16[32,128,256]{2,1,0:T(8,128)(2,1)S(1)} %bitcast.83, f32[4,1,1024]{2,1,0:T(1,128)S(1)} %get-tuple-element.20.m_in, ...), custom_call_target="tpu_custom_call" | custom-call | flops 2147483648 | bytes 3145728 | tf_op jit(solution)/shard_map/pallas_call | solution.py:226
  300.6 20.0 %shard_map.84 = (f32[4,1,1024]{2,1,0:T(1,128)S(1)}, f32[4,1,1024]{2,1,0:T(1,128)S(1)}, f32[4,128,1024]{2,1,0:T(8,128)S(1)}) custom-call(bf16[4,128,1024]{2,1,0:T(8,128)(2,1)S(1)} %reshape.544.q_ref, bf16[1024,256]{1,0:T(8,128)(2,1)S(1)} %copy-done.10, f32[4,1,1024]{2,1,0:T(1,128)S(1)} %get-tuple-element.23.m_in, f32[4,1,1024]{2,1,0:T(1,128)S(1)} %get-tuple-element.24.l_in, ...), custom_call_target="tpu_custom_call" | custom-call | flops 4294967296 | bytes 3145728 | tf_op jit(solution)/shard_map/pallas_call | solution.py:215
  320.6 21.1 %shard_map.85 = (f32[4,1,1024]{2,1,0:T(1,128)S(1)}, f32[4,1,1024]{2,1,0:T(1,128)S(1)}, f32[4,128,1024]{2,1,0:T(8,128)S(1)}) custom-call(s32[32]{0:T(128)S(1)} %reshape.554.seg_ref, bf16[4,128,1024]{2,1,0:T(8,128)(2,1)S(1)} %reshape.544.q_ref, bf16[32,128,256]{2,1,0:T(8,128)(2,1)} %bitcast.24.blocks_ref, f32[4,1,1024]{2,1,0:T(1,128)S(1)} %get-tuple-element.26.m_in, ...), custom_call_target="tpu_custom_call" | custom-call | flops 2147483648 | bytes 3145728 | tf_op jit(solution)/shard_map/pallas_call | solution.py:226
  341.7 11.2 %shard_map.86 = (f32[4,1,1024]{2,1,0:T(1,128)S(1)}, f32[4,1,1024]{2,1,0:T(1,128)S(1)}, f32[4,128,1024]{2,1,0:T(8,128)S(1)}) custom-call(s32[32]{0:T(128)S(1)} %reshape.550.seg_ref, bf16[4,128,1024]{2,1,0:T(8,128)(2,1)S(1)} %reshape.544.q_ref, bf16[32,128,256]{2,1,0:T(8,128)(2,1)S(1)} %bitcast.84, f32[4,1,1024]{2,1,0:T(1,128)S(1)} %get-tuple-element.29.m_in, ...), custom_call_target="tpu_custom_call" | custom-call | flops 2147483648 | bytes 3145728 | tf_op jit(solution)/shard_map/pallas_call | solution.py:226
  355.8 2.8 shard_map.87
  358.7 9.5 %convolution_convert_fusion = bf16[512,4096]{1,0:T(8,128)(2,1)} fusion(bf16[512,1024]{1,0:T(8,128)(2,1)S(1)} %bitcast.86, bf16[1024,4096]{1,0:T(8,128)(2,1)} %param.15), kind=kOutput, calls=%fused_computation.10 | convolution fusion | flops 4297064448 | bytes 13631488 | tf_op jit(solution)/shard_map/dot_general | solution.py:350
  368.2 41.3 %reduce-scatter.2.cloned.1.call-done = bf16[128,4096]{1,0:T(8,128)(2,1)} async-done(((bf16[512,4096]{1,0:T(8,128)(2,1)}), bf16[128,4096]{1,0:T(8,128)(2,1)}) %reduce-scatter.2.cloned.1.call-update) | async-done | bytes 1048592 | tf_op jit(solution)/shard_map/reduce_scatter | solution.py:349
  (142 shorter events, 62.4 us)
Async XLA Ops:
  6.5 7.5 %copy-start = (s32[2048]{0:T(1024)S(1)}, s32[2048]{0:T(1024)}, u32[]{:S(2)}) copy-start(s32[2048]{0:T(1024)} %param.14) | copy-start | bytes 24580
  6.5 57.4 %copy-start.14 = (bf16[32,128,256]{2,1,0:T(8,128)(2,1)S(1)}, bf16[32,128,256]{2,1,0:T(8,128)(2,1)}, u32[]{:S(2)}) copy-start(bf16[32,128,256]{2,1,0:T(8,128)(2,1)} %param.11) | copy-start | bytes 6291460
  6.5 63.0 %collective-permute-start = (bf16[32,128,256]{2,1,0:T(8,128)(2,1)}, bf16[32,128,256]{2,1,0:T(8,128)(2,1)}, u32[]{:S(2)}, u32[]{:S(2)}) collective-permute-start(bf16[32,128,256]{2,1,0:T(8,128)(2,1)} %param.11), channel_id=1, source_target_pairs={{0,32},{4,36},{8,40},{12,44},{16,48},{20,52},{24,56},{28,60},{32,6... | collective-permute-start | bytes 6291464 | tf_op jit(solution)/shard_map/ppermute | solution.py:269
  8.5 63.8 %collective-permute-start.4 = (bf16[32,128,256]{2,1,0:T(8,128)(2,1)}, bf16[32,128,256]{2,1,0:T(8,128)(2,1)}, u32[]{:S(2)}, u32[]{:S(2)}) collective-permute-start(bf16[32,128,256]{2,1,0:T(8,128)(2,1)} %param.11), channel_id=1, source_target_pairs={{0,224},{4,228},{8,232},{12,236},{16,240},{20,244},{24,248},{28,25... | collective-permute-start | bytes 6291464 | tf_op jit(solution)/shard_map/ppermute | solution.py:269
  16.5 46.8 %all-to-all-start = ((s32[64,1,16]{2,1,0:T(1,128)}), s32[64,1,16]{2,1,0:T(1,128)S(1)}, u32[]{:S(2)}, u32[]{:S(2)}) async-start(s32[64,1,16]{2,1,0:T(1,128)} %bitcast.4), calls=%async_computation | async-start | bytes 65536 | tf_op jit(solution)/shard_map/all_to_all | solution.py:300
  65.5 19.5 %all-to-all-start.5 = ((bf16[8,2,128,256]{3,2,1,0:T(8,128)(2,1)}), bf16[8,2,128,256]{3,2,1,0:T(8,128)(2,1)S(1)}, u32[]{:S(2)}, u32[]{:S(2)}) async-start(bf16[8,2,128,256]{3,2,1,0:T(8,128)(2,1)} %bitcast.34), calls=%async_computation.5 | async-start | bytes 2097152 | tf_op jit(solution)/shard_map/all_to_all | solution.py:274
  69.5 49.6 %collective-permute-start.1 = (bf16[32,128,256]{2,1,0:T(8,128)(2,1)}, bf16[32,128,256]{2,1,0:T(8,128)(2,1)}, u32[]{:S(2)}, u32[]{:S(2)}) collective-permute-start(bf16[32,128,256]{2,1,0:T(8,128)(2,1)} %collective-permute-done), channel_id=1, source_target_pairs={{0,32},{4,36},{8,40},{12,44},{16,48},{20,52},{24,56},{28,60},{32,6... | collective-permute-start | bytes 6291464 | tf_op jit(solution)/shard_map/ppermute | solution.py:269
  72.3 49.0 %collective-permute-start.5 = (bf16[32,128,256]{2,1,0:T(8,128)(2,1)}, bf16[32,128,256]{2,1,0:T(8,128)(2,1)}, u32[]{:S(2)}, u32[]{:S(2)}) collective-permute-start(bf16[32,128,256]{2,1,0:T(8,128)(2,1)} %collective-permute-done.4), channel_id=1, source_target_pairs={{0,224},{4,228},{8,232},{12,236},{16,240},{20,244},{24,248},{28,25... | collective-permute-start | bytes 6291464 | tf_op jit(solution)/shard_map/ppermute | solution.py:269
  85.9 41.4 %all-to-all-start.4 = ((bf16[8,2,2,128,256]{4,3,2,1,0:T(8,128)(2,1)}), bf16[8,2,2,128,256]{4,3,2,1,0:T(8,128)(2,1)S(1)}, u32[]{:S(2)}, u32[]{:S(2)}) async-start(bf16[8,2,2,128,256]{4,3,2,1,0:T(8,128)(2,1)} %pad_maximum_fusion.2), calls=%async_computation.4 | async-start | bytes 4194304 | tf_op jit(solution)/shard_map/all_to_all | solution.py:274
  127.3 4.5 %copy-start.2 = (bf16[8,2,2,128,256]{4,3,2,1,0:T(8,128)(2,1)}, bf16[8,2,2,128,256]{4,3,2,1,0:T(8,128)(2,1)S(1)}, u32[]{:S(2)}) copy-start(bf16[8,2,2,128,256]{4,3,2,1,0:T(8,128)(2,1)S(1)} %all-to-all-done.4) | copy-start | bytes 6291460
  127.3 38.7 %all-to-all-start.3 = ((bf16[8,2,2,128,256]{4,3,2,1,0:T(8,128)(2,1)}), bf16[8,2,2,128,256]{4,3,2,1,0:T(8,128)(2,1)}, u32[]{:S(2)}, u32[]{:S(2)}) async-start(bf16[8,2,2,128,256]{4,3,2,1,0:T(8,128)(2,1)} %pad_maximum_fusion.1), calls=%async_computation.3 | async-start | bytes 4194304 | tf_op jit(solution)/shard_map/all_to_all | solution.py:274
  134.0 26.9 %collective-permute-start.8 = (bf16[8,2,128,256]{3,2,1,0:T(8,128)(2,1)S(1)}, bf16[8,2,128,256]{3,2,1,0:T(8,128)(2,1)S(1)}, u32[]{:S(2)}, u32[]{:S(2)}) collective-permute-start(bf16[8,2,128,256]{3,2,1,0:T(8,128)(2,1)S(1)} %bitcast.94), channel_id=1, source_target_pairs={{0,32},{4,36},{8,40},{12,44},{16,48},{20,52},{24,56},{28,60},{32,6... | collective-permute-start | bytes 3145736 | tf_op jit(solution)/shard_map/ppermute | solution.py:269
  137.7 25.5 %collective-permute-start.9 = (bf16[8,2,128,256]{3,2,1,0:T(8,128)(2,1)S(1)}, bf16[8,2,128,256]{3,2,1,0:T(8,128)(2,1)}, u32[]{:S(2)}, u32[]{:S(2)}) collective-permute-start(bf16[8,2,128,256]{3,2,1,0:T(8,128)(2,1)S(1)} %bitcast.95), channel_id=1, source_target_pairs={{0,224},{4,228},{8,232},{12,236},{16,240},{20,244},{24,248},{28,25... | collective-permute-start | bytes 3145736 | tf_op jit(solution)/shard_map/ppermute | solution.py:269
  166.0 105.2 %all-to-all-start.2 = ((bf16[8,2,2,128,256]{4,3,2,1,0:T(8,128)(2,1)}), bf16[8,2,2,128,256]{4,3,2,1,0:T(8,128)(2,1)S(1)}, u32[]{:S(2)}, u32[]{:S(2)}) async-start(bf16[8,2,2,128,256]{4,3,2,1,0:T(8,128)(2,1)} %pad_maximum_fusion), calls=%async_computation.2 | async-start | bytes 4194304 | tf_op jit(solution)/shard_map/all_to_all | solution.py:274
  172.8 15.7 %collective-permute-start.2 = (bf16[4,2,128,256]{3,2,1,0:T(8,128)(2,1)S(1)}, bf16[4,2,128,256]{3,2,1,0:T(8,128)(2,1)}, u32[]{:S(2)}, u32[]{:S(2)}) collective-permute-start(bf16[4,2,128,256]{3,2,1,0:T(8,128)(2,1)S(1)} %bitcast.99), channel_id=1, source_target_pairs={{0,32},{4,36},{8,40},{12,44},{16,48},{20,52},{24,56},{28,60},{32,6... | collective-permute-start | bytes 1572872 | tf_op jit(solution)/shard_map/ppermute | solution.py:269
  175.8 14.2 %collective-permute-start.6 = (bf16[4,2,128,256]{3,2,1,0:T(8,128)(2,1)S(1)}, bf16[4,2,128,256]{3,2,1,0:T(8,128)(2,1)}, u32[]{:S(2)}, u32[]{:S(2)}) collective-permute-start(bf16[4,2,128,256]{3,2,1,0:T(8,128)(2,1)S(1)} %bitcast.98), channel_id=1, source_target_pairs={{0,224},{4,228},{8,232},{12,236},{16,240},{20,244},{24,248},{28,25... | collective-permute-start | bytes 1572872 | tf_op jit(solution)/shard_map/ppermute | solution.py:269
  188.6 80.4 %collective-permute-start.3 = (bf16[4,2,128,256]{3,2,1,0:T(8,128)(2,1)}, bf16[4,2,128,256]{3,2,1,0:T(8,128)(2,1)}, u32[]{:S(2)}, u32[]{:S(2)}) collective-permute-start(bf16[4,2,128,256]{3,2,1,0:T(8,128)(2,1)} %collective-permute-done.2), channel_id=1, source_target_pairs={{0,32},{4,36},{8,40},{12,44},{16,48},{20,52},{24,56},{28,60},{32,6... | collective-permute-start | bytes 1572872 | tf_op jit(solution)/shard_map/ppermute | solution.py:269
  190.0 79.0 %collective-permute-start.7 = (bf16[4,2,128,256]{3,2,1,0:T(8,128)(2,1)}, bf16[4,2,128,256]{3,2,1,0:T(8,128)(2,1)}, u32[]{:S(2)}, u32[]{:S(2)}) collective-permute-start(bf16[4,2,128,256]{3,2,1,0:T(8,128)(2,1)} %collective-permute-done.6), channel_id=1, source_target_pairs={{0,224},{4,228},{8,232},{12,236},{16,240},{20,244},{24,248},{28,25... | collective-permute-start | bytes 1572872 | tf_op jit(solution)/shard_map/ppermute | solution.py:269
  195.3 58.3 %copy-start.11 = (bf16[512,256]{1,0:T(8,128)(2,1)S(1)}, bf16[512,256]{1,0:T(8,128)(2,1)}, u32[]{:S(2)}) copy-start(bf16[512,256]{1,0:T(8,128)(2,1)} %param.9) | copy-start | bytes 786436
  272.6 81.6 %all-to-all-start.1 = ((bf16[8,2,128,256]{3,2,1,0:T(8,128)(2,1)}), bf16[8,2,128,256]{3,2,1,0:T(8,128)(2,1)S(1)}, u32[]{:S(2)}, u32[]{:S(2)}) async-start(bf16[8,2,128,256]{3,2,1,0:T(8,128)(2,1)} %pad_maximum_fusion.3), calls=%async_computation.1 | async-start | bytes 2097152 | tf_op jit(solution)/shard_map/all_to_all | solution.py:274
  276.2 133.3 %reduce-scatter.2.cloned.1.call-start = ((), (), s32[]{:S(2)}) async-start(), calls=%async_computation.7 | async-start | bytes 5242880 | tf_op jit(solution)/shard_map/reduce_scatter | solution.py:349
  279.4 21.1 %copy-start.10 = (bf16[1024,256]{1,0:T(8,128)(2,1)S(1)}, bf16[1024,256]{1,0:T(8,128)(2,1)}, u32[]{:S(2)}) copy-start(bf16[1024,256]{1,0:T(8,128)(2,1)} %all_gather.3.prompt_ref) | copy-start | bytes 1572868
  320.6 21.1 %copy-start.5 = (bf16[8,2,2,128,256]{4,3,2,1,0:T(8,128)(2,1)S(1)}, bf16[8,2,2,128,256]{4,3,2,1,0:T(8,128)(2,1)}, u32[]{:S(2)}) copy-start(bf16[8,2,2,128,256]{4,3,2,1,0:T(8,128)(2,1)} %copy-done.4) | copy-start | bytes 6291460
  368.2 41.3 %copy-start.1 = (s32[2048]{0:T(1024)S(1)}, s32[2048]{0:T(1024)}, u32[]{:S(2)}) copy-start(s32[2048]{0:T(1024)} %param.14) | copy-start | bytes 24580
  (9 other events, 15.0 us)
Sparse Core Ops, SparseCore 0:
  368.3 41.1 reduce-scatter.1

commit v2 on v1

v2 whole, which is shorter than its diff:
```python
import functools

import jax
import jax.numpy as jnp
from jax import lax
from jax.experimental import pallas as pl
from jax.experimental.pallas import tpu as pltpu
from jax.sharding import PartitionSpec as P

Y_SIZE = 4
CORES = 2
LANES = Y_SIZE * CORES
LOG2E = 1.4426950408889634
TILE = 256
PROJECT_TILE = 2048
SMALL = pl.CostEstimate(flops=1 << 16, bytes_accessed=1 << 16, transcendentals=0)
LARGE = pl.CostEstimate(flops=0, bytes_accessed=1 << 31, transcendentals=0)


def absorb(seg, keys, values, q_ref, m_ref, l_ref, acc_ref, scale, mask=None, first=False):
    factor = scale * LOG2E
    tiles = [slice(at, at + TILE) for at in range(0, q_ref.shape[2], TILE)]
    scores = [jnp.dot(keys, q_ref[seg, :, t], preferred_element_type=jnp.float32) for t in tiles]
    if mask is not None:
        scores = [jnp.where(mask, x, jnp.float32(-1e30)) for x in scores]
    tops = [jnp.max(x, axis=0, keepdims=True) for x in scores]
    if not first:
        before = [m_ref[seg, :, t] for t in tiles]
        tops = [jnp.maximum(b, x) for b, x in zip(before, tops)]
        shrinks = [jnp.exp2((b - x) * factor) for b, x in zip(before, tops)]
    probs = [jnp.exp2((x - top) * factor) for x, top in zip(scores, tops)]
    totals = [jnp.sum(p, axis=0, keepdims=True) for p in probs]
    sums = [
        lax.dot_general(
            values,
            p.astype(jnp.bfloat16),
            (((0,), (0,)), ((), ())),
            preferred_element_type=jnp.float32,
        )
        for p in probs
    ]
    if not first:
        totals = [n + l_ref[seg, :, t] * f for n, t, f in zip(totals, tiles, shrinks)]
        sums = [n + acc_ref[seg, :, t] * f for n, t, f in zip(sums, tiles, shrinks)]
    for t, top, total, summed in zip(tiles, tops, totals, sums):
        m_ref[seg, :, t] = top
        l_ref[seg, :, t] = total
        acc_ref[seg, :, t] = summed


def absorb_blocks(seg_ref, blocks_ref, q_ref, m_ref, l_ref, acc_ref, list_ref, count_ref, scale):
    places = seg_ref.shape[0]
    segs = q_ref.shape[0]
    head_dim = q_ref.shape[1]
    for seg in range(segs):
        count_ref[seg] = 0

    def place(at, carry):
        seg = seg_ref[at]

        @pl.when(seg >= 0)
        def _():
            used = count_ref[seg]
            list_ref[seg * places + used] = at
            count_ref[seg] = used + 1

        return carry

    lax.fori_loop(0, places, place, 0)

    def per_segment(seg, carry):
        count = count_ref[seg]

        def take(at, how_many):
            places_of = [list_ref[seg * places + at + i] for i in range(how_many)]
            found = [blocks_ref[p] for p in places_of]
            both = found[0] if how_many == 1 else jnp.concatenate(found, axis=0)
            absorb(seg, both[:, :head_dim], both[:, head_dim:], q_ref, m_ref, l_ref, acc_ref, scale)

        def quad(step, inner):
            take(4 * step, 4)
            return inner

        lax.fori_loop(0, count // 4, quad, 0)
        rest = count // 4 * 4

        @pl.when(count % 4 >= 2)
        def _():
            take(rest, 2)

        @pl.when(count % 2 == 1)
        def _():
            take(count - 1, 1)

        return carry

    lax.fori_loop(0, segs, per_segment, 0)


def own_kernel(scale, q_ref, own_ref, m_ref, l_ref, acc_ref):
    head_dim = q_ref.shape[1]
    seg_len = own_ref.shape[1]
    key_at = lax.broadcasted_iota(jnp.int32, (seg_len, TILE), 0)
    query_at = lax.broadcasted_iota(jnp.int32, (seg_len, TILE), 1) % seg_len
    causal = query_at >= key_at

    def own(seg, carry):
        keys, values = own_ref[seg, :, :head_dim], own_ref[seg, :, head_dim:]
        absorb(seg, keys, values, q_ref, m_ref, l_ref, acc_ref, scale, mask=causal, first=True)
        return carry

    lax.fori_loop(0, q_ref.shape[0], own, 0)


def carry_in(old, new):
    for source, target in zip(old, new):
        target[...] = source[...]


def chunk_kernel(scale, shared, seg_ref, q_ref, blocks_ref, m_in, l_in, acc_in, m_ref, l_ref, acc_ref, list_ref, count_ref):
    carry_in((m_in, l_in, acc_in), (m_ref, l_ref, acc_ref))
    absorb_blocks(seg_ref, blocks_ref, q_ref, m_ref, l_ref, acc_ref, list_ref, count_ref, scale)
    head_dim = q_ref.shape[1]

    def step(seg, carry):
        for at in range(0, len(shared), 4):
            found = jnp.concatenate([blocks_ref[p] for p in shared[at : at + 4]], axis=0)
            keys, values = found[:, :head_dim], found[:, head_dim:]
            absorb(seg, keys, values, q_ref, m_ref, l_ref, acc_ref, scale)
        return carry

    if shared:
        lax.fori_loop(0, q_ref.shape[0], step, 0)


def last_kernel(scale, seg_ref, x_ref, q_ref, blocks_ref, m_in, l_in, acc_in, *refs):
    outs, (m_ref, l_ref, acc_ref, list_ref, count_ref) = refs[:-5], refs[-5:]
    carry_in((m_in, l_in, acc_in), (m_ref, l_ref, acc_ref))
    absorb_blocks(seg_ref, blocks_ref, q_ref, m_ref, l_ref, acc_ref, list_ref, count_ref, scale)
    seg_len = outs[0].shape[0]
    head_dim = q_ref.shape[1]
    group = q_ref.shape[2] // seg_len
    segs = q_ref.shape[0]

    for step, out_ref in enumerate(outs):
        seg = (x_ref[0] + step) % segs
        for g in range(group):
            cols = slice(g * seg_len, (g + 1) * seg_len)
            value = acc_ref[seg, :, cols] / l_ref[seg, :, cols]
            out_ref[:, g * head_dim : (g + 1) * head_dim] = value.T.astype(jnp.bfloat16)


def pick_kernel(sources, n_in, rows_ref, *refs):
    inputs, outputs, sems = refs[:n_in], refs[n_in:-1], refs[-1]
    base = 0
    for number, (names, out_ref) in enumerate(zip(sources, outputs)):

        def step(at, carry, names=names, out_ref=out_ref, base=base, number=number):
            for inner, name in enumerate(names):
                place = at * len(names) + inner
                pltpu.make_async_copy(
                    inputs[name].at[rows_ref[base + place]], out_ref.at[place], sems.at[number]
                ).start()
            return carry

        lax.fori_loop(0, out_ref.shape[0] // len(names), step, 0)
        base += out_ref.shape[0]
    for number, out_ref in enumerate(outputs):
        pltpu.make_async_copy(out_ref, out_ref, sems.at[number]).wait()


def project_kernel(kind, first, c_ref, *refs):
    out_ref = refs[-1]
    refs = list(refs[:-1])
    total = None if first else refs.pop(0)[...]
    if kind == "whole":
        pairs = [(refs[0][...], refs[1])]
    else:
        right, left = refs[0][...], refs[1][...]
        even = c_ref[0] == 0
        pairs = [(jnp.where(even, right, left), refs[2]), (jnp.where(even, left, right), refs[3])]
    for rows, weight_ref in pairs:
        product = jnp.dot(rows, weight_ref[...], preferred_element_type=jnp.float32)
        total = product if total is None else total + product
    out_ref[...] = total.astype(out_ref.dtype)


VMEM = pl.BlockSpec(memory_space=pltpu.VMEM)
SMEM = pl.BlockSpec(memory_space=pltpu.SMEM)
ANY = pl.BlockSpec(memory_space=pl.ANY)


def state_shapes(q):
    segs, head_dim, columns = q.shape
    return [
        jax.ShapeDtypeStruct((segs, 1, columns), jnp.float32),
        jax.ShapeDtypeStruct((segs, 1, columns), jnp.float32),
        jax.ShapeDtypeStruct((segs, head_dim, columns), jnp.float32),
    ]


def params():
    return pltpu.CompilerParams(vmem_limit_bytes=40 * 1024 * 1024)


def tables(places, segs):
    return [pltpu.SMEM((segs * places,), jnp.int32), pltpu.SMEM((segs,), jnp.int32)]


def attend_own(q, own, scale):
    return pl.pallas_call(
        functools.partial(own_kernel, scale),
        out_shape=state_shapes(q),
        in_specs=[VMEM, VMEM],
        out_specs=[VMEM] * 3,
        compiler_params=params(),
        cost_estimate=SMALL,
    )(q, own)


def attend_chunk(q, seg_of, blocks, state, scale, shared=()):
    return pl.pallas_call(
        functools.partial(chunk_kernel, scale, shared),
        out_shape=state_shapes(q),
        in_specs=[SMEM] + [VMEM] * 5,
        out_specs=[VMEM] * 3,
        scratch_shapes=tables(seg_of.shape[0], q.shape[0]),
        compiler_params=params(),
        cost_estimate=SMALL,
    )(seg_of, q, blocks, *state)


def attend_last(q, seg_of, blocks, state, x, scale):
    segs, head_dim, columns = q.shape
    seg_len = blocks.shape[1]
    group = columns // seg_len
    return pl.pallas_call(
        functools.partial(last_kernel, scale),
        out_shape=[jax.ShapeDtypeStruct((seg_len, group * head_dim), jnp.bfloat16)] * segs,
        in_specs=[SMEM, SMEM] + [VMEM] * 5,
        out_specs=[VMEM] * segs,
        scratch_shapes=[pltpu.VMEM(s.shape, s.dtype) for s in state_shapes(q)]
        + tables(seg_of.shape[0], segs),
        compiler_params=params(),
        cost_estimate=SMALL,
    )(seg_of, x, q, blocks, *state)


def pick(plan, buffers, told=None):
    block = buffers[0].shape[1:]
    out = pl.pallas_call(
        functools.partial(pick_kernel, tuple(names for names, _ in plan), len(buffers)),
        out_shape=[
            jax.ShapeDtypeStruct((rows.size,) + block, buffers[0].dtype) for _, rows in plan
        ],
        in_specs=[SMEM] + [ANY] * len(buffers),
        out_specs=[VMEM] * len(plan),
        scratch_shapes=[pltpu.SemaphoreType.DMA((len(plan),))],
        compiler_params=params(),
        cost_estimate=told or SMALL,
    )(jnp.concatenate([rows.reshape(-1) for _, rows in plan]), *buffers)
    return [x.reshape(rows.shape + block) for x, (_, rows) in zip(out, plan)]


def project(c, kind, blocks, weights, total, dtype):
    rows = blocks[0].shape[0]
    columns = weights[0].shape[1]
    tile = PROJECT_TILE
    wide = pl.BlockSpec((rows, tile), lambda at: (0, at))
    operands = [c] + ([] if total is None else [total]) + blocks + weights
    specs = [SMEM] + ([] if total is None else [wide])
    specs += [pl.BlockSpec(x.shape, lambda at: (0, 0)) for x in blocks]
    specs += [pl.BlockSpec((w.shape[0], tile), lambda at: (0, at)) for w in weights]
    depth = sum(w.shape[0] for w in weights)
    return pl.pallas_call(
        functools.partial(project_kernel, kind, total is None),
        out_shape=jax.ShapeDtypeStruct((rows, columns), dtype),
        grid=(columns // tile,),
        in_specs=specs,
        out_specs=wide,
        compiler_params=params(),
        cost_estimate=pl.CostEstimate(
            flops=2 * rows * depth * columns, bytes_accessed=2 * depth * columns, transcendentals=0
        ),
    )(*operands)


def together(*arrays):
    return lax.optimization_barrier(arrays)


def per_device(queries, new_kv, prompt_kv, pool, parents, lengths, location, out_weight):
    tok_rows = queries.shape[0]
    seg_dev, max_anc = parents.shape
    head_dim = prompt_kv.shape[1] // 2
    group = queries.shape[1] // head_dim
    seg_len = tok_rows // seg_dev
    blocks = pool.shape[0]
    scale = head_dim ** (-0.5)
    n_leaf = lax.axis_size("leaf")
    n_head = lax.axis_size("head")
    planes = n_leaf // LANES
    capacity = 2
    me = lax.axis_index("leaf")
    plane = me // LANES
    core = me % CORES

    def along_z(x, step):
        pairs = [(d, (d + step * LANES) % n_leaf) for d in range(n_leaf)]
        return lax.ppermute(x, "leaf", pairs)

    def along_x(x, step):
        return lax.ppermute(x, "head", [(d, (d + step) % n_head) for d in range(n_head)])

    def other_core(x):
        return lax.ppermute(x, "leaf", [(d, d ^ 1) for d in range(n_leaf)])

    in_plane = [[p * LANES + lane for lane in range(LANES)] for p in range(planes)]

    def spread(x):
        return lax.all_to_all(x, "leaf", 0, 0, tiled=True, axis_index_groups=in_plane)

    up1 = along_z(pool, 1)
    down1 = along_z(pool, -1)

    n_all = n_leaf * n_head

    def by_core(x):
        pairs = []
        for d in range(n_all):
            leaf, head = divmod(d, n_head)
            step = -1 if leaf % CORES == 0 else 1
            pairs.append((d, leaf * n_head + (head + step) % n_head))
        return lax.ppermute(x, ("leaf", "head"), pairs)

    weight1 = by_core(out_weight)

    slots = seg_dev * max_anc
    stored = location[parents].reshape(-1)
    live = (jnp.arange(max_anc)[None, :] < lengths[:, None]).reshape(-1)
    owner = jnp.where(live, stored // blocks, -1)
    row = stored % blocks
    order = jnp.arange(slots)
    rank = jnp.sum(
        (owner[:, None] == owner[None, :]) & (order[:, None] > order[None, :]), axis=1
    )
    dist = (plane - owner // LANES) % planes
    cell = jnp.where(live, (dist * LANES + owner % LANES) * capacity + rank, -1)
    hit = cell[None, :] == jnp.arange(n_leaf * capacity)[:, None]
    wanted = jnp.sum(jnp.where(hit, row[None, :], 0), axis=1).astype(jnp.int32)
    seg_of = jnp.sum(jnp.where(hit, (order // max_anc + 1)[None, :], 0), axis=1) - 1
    seg_of = seg_of.astype(jnp.int32).reshape(planes, LANES, capacity)
    per_lane = jnp.transpose(wanted.reshape(planes, LANES, capacity), (1, 0, 2))
    here = spread(per_lane.reshape(LANES, 1, planes * capacity))
    here = here.reshape(LANES, planes, capacity)

    q = jnp.transpose(
        queries.reshape(seg_dev, seg_len, group, head_dim), (0, 3, 2, 1)
    ).reshape(seg_dev, head_dim, group * seg_len)
    own = new_kv.reshape(seg_dev, seg_len, 2 * head_dim)
    state = attend_own(q, own, scale)
    here, *state = together(here, *state)

    def segs_at(dists, more=0):
        parts = [seg_of[d] for d in dists] + [jnp.full((LANES, more), -1, jnp.int32)] * bool(more)
        return jnp.concatenate(parts, axis=1).reshape(-1)

    def flat(x):
        return x.reshape((-1,) + x.shape[-2:])

    prompt_rows, width = prompt_kv.shape
    table = here.reshape(1, -1).astype(prompt_kv.dtype)
    table = jnp.pad(table, ((0, prompt_rows - 1), (0, width - table.shape[1])))
    notice = jnp.concatenate([prompt_kv, table], axis=0)
    same_lane = [[p * LANES + lane for p in range(planes)] for lane in range(LANES)]
    notices = lax.all_to_all(
        jnp.broadcast_to(notice[None], (planes,) + notice.shape),
        "leaf",
        0,
        0,
        tiled=True,
        axis_index_groups=same_lane,
    )
    up2 = along_z(up1, 1)
    down2 = along_z(down1, -1)
    lane_prompt = notices[:, :prompt_rows].reshape(1, planes * prompt_rows, width)
    asked = notices[:, prompt_rows, : LANES * planes * capacity].astype(jnp.int32)
    asked = asked.reshape(planes, LANES, planes, capacity)
    asked = lax.dynamic_slice_in_dim(jnp.concatenate([asked, asked], axis=0), plane, planes, 0)

    zero = jnp.zeros((LANES, 1), jnp.int32)
    rows01 = jnp.concatenate([here[:, 0], here[:, 1], here[:, planes - 1], zero], axis=1)
    plan01 = ((0, 0, 1, 1, 2, 2, 3), rows01)
    got01 = spread(pick([plan01], [pool, up1, down1, lane_prompt])[0])

    half = LANES // 2
    ask_up = jnp.concatenate([asked[1, :, 3], asked[2, :half, 4]], axis=0)
    ask_down = jnp.concatenate(
        [asked[planes - 1, :, planes - 3], asked[planes - 2, half:, 4]], axis=0
    )
    rows2 = jnp.concatenate([here[:, 2], here[:, planes - 2]], axis=1)
    send_up, send_down, rest = pick(
        [((0,), ask_up), ((1,), ask_down), ((0, 0, 1, 1), rows2)], [up2, down2], LARGE
    )
    up3 = along_z(send_up, 1)
    down3 = along_z(send_down, -1)
    rest, got01, weight1 = together(rest, got01, weight1)
    got2 = spread(rest)
    weight2 = by_core(weight1)
    weight1_too = other_core(weight1)
    every = 3 * capacity + 1
    prompts = tuple(range(every - 1, LANES * every, every))
    state = attend_chunk(
        q, segs_at([0, 1, planes - 1], 1), flat(got01), state, scale, shared=prompts
    )

    up3, down3, got2, *state = together(up3, down3, got2, *state)
    def counted(start, stop):
        return jnp.arange(start * capacity, stop * capacity, dtype=jnp.int32)

    in_turn = jnp.concatenate([counted(0, LANES).reshape(LANES, capacity)] * 2, axis=1)
    rest, far_up, far_down = pick(
        [
            ((0, 0, 1, 1), in_turn),
            ((0,), counted(LANES, LANES + half)),
            ((1,), counted(LANES, LANES + half)),
        ],
        [flat(up3), flat(down3)],
    )
    far_up4 = along_z(far_up, 1).reshape((half, capacity) + pool.shape[1:])
    far_down4 = along_z(far_down, -1).reshape((half, capacity) + pool.shape[1:])
    got3 = spread(rest)
    state = attend_chunk(q, segs_at([2, planes - 2]), flat(got2), state, scale)

    got4 = spread(jnp.concatenate([far_up4, far_down4], axis=0))
    state = attend_chunk(q, segs_at([3, planes - 3]), flat(got3), state, scale)

    got4, weight1_too, *state = together(got4, weight1_too, *state)
    x = lax.axis_index("head").astype(jnp.int32).reshape(1)
    keep, to_up, to_far, to_down = attend_last(q, segs_at([4]), flat(got4), state, x, scale)

    from_far = along_x(to_far, 2)
    from_down = along_x(to_up, 1)
    from_up = along_x(to_down, -1)
    c = core.astype(jnp.int32).reshape(1)
    total = project(c, "whole", [keep], [out_weight], None, jnp.float32)
    from_down, from_up, total = together(from_down, from_up, total)
    total = project(
        c, "either", [from_up, from_down], [weight1, weight1_too], total, jnp.float32
    )
    return project(c, "whole", [from_far], [weight2], total, jnp.bfloat16)


def solution(mesh):
    return jax.shard_map(
        per_device,
        mesh=mesh,
        in_specs=(
            P("leaf", "head"),
            P("leaf", "head"),
            P("leaf", "head"),
            P("leaf", None, "head"),
            P("leaf", None),
            P("leaf"),
            P(),
            P("head", None),
        ),
        out_specs=P(("leaf", "head"), None),
        check_vma=False,
    )
```

time: 420 us -> 266 us (0.63)
  blocking collectives: 54.4 us -> 0 us
  waiting for transfers between devices: 148 us -> 113 us
  Pallas kernels: 89 us -> 70.5 us
  local copies, waits for them, and re-layouts: 41.2 us -> 27.6 us
  between operations: 13.9 us -> 0.39 us
  matrix products: 9.48 us -> 0 us
  other arithmetic: 11.3 us -> 3.75 us
    all_gather x1 -> x0, blocking collectives: 54.4 us -> none  [per_device(): prompt = lax.all_gather(prompt_kv, 'leaf', axis=0, tiled=True)]
    reduce_scatter x1 -> x0, waiting for transfers between devices: 41.3 us -> none  [per_device(): lax.psum_scatter(jnp.dot(attended.reshape(tok_rows, group * head_dim), ou...]
    gather x9 -> x0, local copies, waits for them, and re-layouts: 20.1 us -> none  [pick(): return buffer[rows.reshape(-1)].reshape(rows.shape + buffer.shape[1:])]
    pallas_call x6 -> x11, Pallas kernels: 89 us -> 70.5 us  [the longest x3 35.2 us: attend_chunk(): pl.pallas_call(functools.partial(chunk_kernel, scale, shared), out_shape=...]
    all_to_all x1, waiting for transfers between devices: 37.3 us -> 26.7 us  [per_device(): lax.all_to_all(jnp.broadcast_to(notice[None], (planes,) + notice.shape),...]
    dot_general x1 -> x0, matrix products: 9.48 us -> none  [per_device(): jnp.dot(attended.reshape(tok_rows, group * head_dim), out_weight, preferr...]
    ppermute x10 -> x8, waiting for transfers between devices: 63.5 us -> 72.6 us  [along_z(): return lax.ppermute(x, 'leaf', pairs)]
    another operation x6 -> x0, other arithmetic: 7.17 us -> none  [the longest x1 2.8 us: per_device(): got3 = spread(jnp.stack([up3, down3], axis=1))]
  transfers between devices with their start and end apart: 17 -> 20, of which waited for: 8 -> 7; matrix products, arithmetic and copies ran while one was open for 10% -> 5% of each run, Pallas kernels for 21% -> 25%
where the time goes in v2:
time: 266 us; the launch traced here: 265 us
  waiting for transfers between devices  113 us (42%)
  Pallas kernels  70.5 us (27%)
  starting transfers between devices  50 us (19%)
  local copies, waits for them, and re-layouts  27.6 us (10%)
  other arithmetic  3.75 us (1%)
    ppermute x8, waiting for transfers between devices, along_z(): return lax.ppermute(x, 'leaf', pairs)  72.6 us
    pallas_call x3, Pallas kernels, attend_chunk(): pl.pallas_call(functools.partial(chunk_kernel, scale, shared), out_shape=...  35.2 us
    all_to_all x1, waiting for transfers between devices, per_device(): lax.all_to_all(jnp.broadcast_to(notice[None], (planes,) + notice.shape),...  26.7 us
    all_to_all x5, starting transfers between devices, spread(): lax.all_to_all(x, 'leaf', 0, 0, tiled=True, axis_index_groups=in_plane)  22.1 us
    unnamed x40, local copies, waits for them, and re-layouts  18.7 us
    ppermute x8, starting transfers between devices, along_z(): return lax.ppermute(x, 'leaf', pairs)  15.7 us
    pallas_call x3, Pallas kernels, project(): pl.pallas_call(functools.partial(project_kernel, kind, total is None), ou...  14.6 us
    pallas_call x3, Pallas kernels, pick(): pl.pallas_call(functools.partial(pick_kernel, tuple((names for names, _ i...  11.6 us
  transfers between devices with their start and end apart: 20, of which 7 were waited for; matrix products, arithmetic and copies ran while one was open for 5% of the time, Pallas kernels for 25%

profile of v2, /device:TPU:6, one launch (start us, length us, event | category | flops | bytes accessed | tf_op | source)
XLA Modules:
  0.0 264.9 jit_solution(3943897785192468592)
XLA Ops:
  2.8 3.9 %collective-permute-start.2 = (bf16[32,128,256]{2,1,0:T(8,128)(2,1)}, bf16[32,128,256]{2,1,0:T(8,128)(2,1)}, u32[]{:S(2)}, u32[]{:S(2)}) collective-permute-start(bf16[32,128,256]{2,1,0:T(8,128)(2,1)} %refs_0_.1), channel_id=1, source_target_pairs={{0,224},{4,228},{8,232},{12,236},{16,240},{20,244},{24,248},{28,25... | collective-permute-start | bytes 6291464 | tf_op jit(solution)/shard_map/ppermute | solution.py:310
  10.7 4.5 %all-to-all-start = ((s32[8,1,16]{2,1,0:T(1,128)}), s32[8,1,16]{2,1,0:T(1,128)S(1)}, u32[]{:S(2)}, u32[]{:S(2)}) async-start(s32[8,1,16]{2,1,0:T(1,128)} %copy.44), calls=%async_computation | async-start | bytes 8192 | tf_op jit(solution)/shard_map/all_to_all | solution.py:321
  23.4 5.8 %all-to-all-start.1 = ((bf16[8,32,256]{2,1,0:T(8,128)(2,1)}), bf16[8,32,256]{2,1,0:T(8,128)(2,1)S(1)}, u32[]{:S(2)}, u32[]{:S(2)}) async-start(bf16[8,32,256]{2,1,0:T(8,128)(2,1)} %broadcast_in_dim.44), calls=%async_computation.1 | async-start | bytes 262144 | tf_op jit(solution)/shard_map/all_to_all | solution.py:376
  29.4 26.7 %all-to-all-done.1 = bf16[8,32,256]{2,1,0:T(8,128)(2,1)S(1)} async-done(((bf16[8,32,256]{2,1,0:T(8,128)(2,1)}), bf16[8,32,256]{2,1,0:T(8,128)(2,1)S(1)}, u32[]{:S(2)}, u32[]{:S(2)}) %all-to-all-start.1) | async-done | bytes 131104 | tf_op jit(solution)/shard_map/all_to_all | solution.py:376
  56.2 3.6 %shard_map.84 = bf16[56,128,256]{2,1,0:T(8,128)(2,1)S(1)} custom-call(s32[56]{0:T(128)S(1)} %reshape.358.rows_ref, bf16[32,128,256]{2,1,0:T(8,128)(2,1)S(1)} %copy-done.4, bf16[32,128,256]{2,1,0:T(8,128)(2,1)} %collective-permute-done.refs_1_, bf16[32,128,256]{2,1,0:T(8,128)(2,1)} %collective-permute-done.2.refs_2_, bf16[1,128,256]{2,1,0:T(8,128)(2,1)S(1)} %bitcast.47), custom_call_target="tpu_custom_call" | custom-call | flops 65536 | bytes 65536 | tf_op jit(solution)/shard_map/pallas_call | solution.py:251
  61.6 4.5 %all-to-all-start.2 = ((bf16[8,7,128,256]{3,2,1,0:T(8,128)(2,1)}), bf16[8,7,128,256]{3,2,1,0:T(8,128)(2,1)}, u32[]{:S(2)}, u32[]{:S(2)}) async-start(bf16[8,7,128,256]{3,2,1,0:T(8,128)(2,1)} %bitcast.43), calls=%async_computation.2 | async-start | bytes 7340032 | tf_op jit(solution)/shard_map/all_to_all | solution.py:321
  66.2 3.2 %collective-permute-start.1 = (bf16[32,128,256]{2,1,0:T(8,128)(2,1)}, bf16[32,128,256]{2,1,0:T(8,128)(2,1)S(1)}, u32[]{:S(2)}, u32[]{:S(2)}) collective-permute-start(bf16[32,128,256]{2,1,0:T(8,128)(2,1)} %collective-permute-done.refs_1_), channel_id=1, source_target_pairs={{0,32},{4,36},{8,40},{12,44},{16,48},{20,52},{24,56},{28,60},{32,6... | collective-permute-start | bytes 6291464 | tf_op jit(solution)/shard_map/ppermute | solution.py:310
  71.1 44.4 %collective-permute-done.1.refs_0_ = bf16[32,128,256]{2,1,0:T(8,128)(2,1)S(1)} collective-permute-done((bf16[32,128,256]{2,1,0:T(8,128)(2,1)}, bf16[32,128,256]{2,1,0:T(8,128)(2,1)S(1)}, u32[]{:S(2)}, u32[]{:S(2)}) %collective-permute-start.1) | collective-permute-done | bytes 2097184 | tf_op jit(solution)/shard_map/ppermute | solution.py:310
  117.3 5.4 %shard_map.83 = (bf16[24,128,256]{2,1,0:T(8,128)(2,1)S(1)}, bf16[24,128,256]{2,1,0:T(8,128)(2,1)S(1)}, bf16[32,128,256]{2,1,0:T(8,128)(2,1)S(1)}) custom-call(s32[80]{0:T(128)S(1)} %pad_add_fusion.7.rows_ref, bf16[32,128,256]{2,1,0:T(8,128)(2,1)S(1)} %collective-permute-done.1.refs_0_, bf16[32,128,256]{2,1,0:T(8,128)(2,1)} %collective-permute-done.3.refs_1_), custom_call_target="tpu_custom_call" | custom-call | bytes 2147483648 | tf_op jit(solution)/shard_map/pallas_call | solution.py:251
  128.0 4.4 %all-to-all-start.3 = ((bf16[8,4,128,256]{3,2,1,0:T(8,128)(2,1)}), bf16[8,4,128,256]{3,2,1,0:T(8,128)(2,1)S(1)}, u32[]{:S(2)}, u32[]{:S(2)}) async-start(bf16[8,4,128,256]{3,2,1,0:T(8,128)(2,1)} %bitcast.45), calls=%async_computation.3 | async-start | bytes 4194304 | tf_op jit(solution)/shard_map/all_to_all | solution.py:321
  138.1 17.4 %shard_map.85 = (f32[4,1,1024]{2,1,0:T(1,128)S(1)}, f32[4,1,1024]{2,1,0:T(1,128)S(1)}, f32[4,128,1024]{2,1,0:T(8,128)S(1)}) custom-call(s32[56]{0:T(128)S(1)} %reshape.361.seg_ref, bf16[4,128,1024]{2,1,0:T(8,128)(2,1)S(1)} %reshape.343.q_ref, bf16[56,128,256]{2,1,0:T(8,128)(2,1)} %bitcast.22.blocks_ref, f32[4,1,1024]{2,1,0:T(1,128)S(1)} %get-tuple-element.57.m_in, ...), custom_call_target="tpu_custom_call" | custom-call | flops 65536 | bytes 65536 | tf_op jit(solution)/shard_map/pallas_call | solution.py:222
  156.9 13.9 %collective-permute-done.4 = bf16[12,2,128,256]{3,2,1,0:T(8,128)(2,1)} collective-permute-done((bf16[12,2,128,256]{3,2,1,0:T(8,128)(2,1)}, bf16[12,2,128,256]{3,2,1,0:T(8,128)(2,1)}, u32[]{:S(2)}, u32[]{:S(2)}) %collective-permute-start.4) | collective-permute-done | bytes 1572896 | tf_op jit(solution)/shard_map/ppermute | solution.py:310
  176.2 4.4 %all-to-all-start.5 = ((bf16[8,4,128,256]{3,2,1,0:T(8,128)(2,1)}), bf16[8,4,128,256]{3,2,1,0:T(8,128)(2,1)}, u32[]{:S(2)}, u32[]{:S(2)}) async-start(bf16[8,4,128,256]{3,2,1,0:T(8,128)(2,1)} %bitcast.46), calls=%async_computation.5 | async-start | bytes 4194304 | tf_op jit(solution)/shard_map/all_to_all | solution.py:321
  180.7 3.2 %collective-permute-start.8 = (bf16[8,128,256]{2,1,0:T(8,128)(2,1)}, bf16[8,128,256]{2,1,0:T(8,128)(2,1)S(1)}, u32[]{:S(2)}, u32[]{:S(2)}) collective-permute-start(bf16[8,128,256]{2,1,0:T(8,128)(2,1)} %copy-done.14), channel_id=1, source_target_pairs={{0,224},{4,228},{8,232},{12,236},{16,240},{20,244},{24,248},{28,25... | collective-permute-start | bytes 1572872 | tf_op jit(solution)/shard_map/ppermute | solution.py:310
  183.9 12.5 %collective-permute-done.7 = bf16[8,128,256]{2,1,0:T(8,128)(2,1)S(1)} collective-permute-done((bf16[8,128,256]{2,1,0:T(8,128)(2,1)}, bf16[8,128,256]{2,1,0:T(8,128)(2,1)S(1)}, u32[]{:S(2)}, u32[]{:S(2)}) %collective-permute-start.7) | collective-permute-done | bytes 524320 | tf_op jit(solution)/shard_map/ppermute | solution.py:310
  197.5 10.5 %all-to-all-done.5 = bf16[8,4,128,256]{3,2,1,0:T(8,128)(2,1)} async-done(((bf16[8,4,128,256]{3,2,1,0:T(8,128)(2,1)}), bf16[8,4,128,256]{3,2,1,0:T(8,128)(2,1)}, u32[]{:S(2)}, u32[]{:S(2)}) %all-to-all-start.5) | async-done | bytes 2097184 | tf_op jit(solution)/shard_map/all_to_all | solution.py:321
  208.0 4.3 %all-to-all-start.4 = ((bf16[8,2,128,256]{3,2,1,0:T(8,128)(2,1)}), bf16[8,2,128,256]{3,2,1,0:T(8,128)(2,1)}, u32[]{:S(2)}, u32[]{:S(2)}) async-start(bf16[8,2,128,256]{3,2,1,0:T(8,128)(2,1)} %pad_maximum_fusion), calls=%async_computation.4 | async-start | bytes 2097152 | tf_op jit(solution)/shard_map/all_to_all | solution.py:321
  214.5 7.1 %shard_map.87 = (f32[4,1,1024]{2,1,0:T(1,128)S(1)}, f32[4,1,1024]{2,1,0:T(1,128)S(1)}, f32[4,128,1024]{2,1,0:T(8,128)S(1)}) custom-call(s32[32]{0:T(128)S(1)} %reshape.370.seg_ref, bf16[4,128,1024]{2,1,0:T(8,128)(2,1)S(1)} %reshape.343.q_ref, bf16[32,128,256]{2,1,0:T(8,128)(2,1)S(1)} %bitcast.44, f32[4,1,1024]{2,1,0:T(1,128)S(1)} %get-tuple-element.70.m_in, ...), custom_call_target="tpu_custom_call" | custom-call | flops 65536 | bytes 65536 | tf_op jit(solution)/shard_map/pallas_call | solution.py:222
  221.5 10.7 %shard_map.88 = (f32[4,1,1024]{2,1,0:T(1,128)S(1)}, f32[4,1,1024]{2,1,0:T(1,128)S(1)}, f32[4,128,1024]{2,1,0:T(8,128)S(1)}) custom-call(s32[32]{0:T(128)S(1)} %reshape.367.seg_ref, bf16[4,128,1024]{2,1,0:T(8,128)(2,1)S(1)} %reshape.343.q_ref, bf16[32,128,256]{2,1,0:T(8,128)(2,1)} %bitcast.28.blocks_ref, f32[4,1,1024]{2,1,0:T(1,128)S(1)} %get-tuple-element.73.m_in, ...), custom_call_target="tpu_custom_call" | custom-call | flops 65536 | bytes 65536 | tf_op jit(solution)/shard_map/pallas_call | solution.py:222
  232.2 7.2 %shard_map.89 = (bf16[128,1024]{1,0:T(8,128)(2,1)S(1)}, bf16[128,1024]{1,0:T(8,128)(2,1)}, bf16[128,1024]{1,0:T(8,128)(2,1)S(1)}, bf16[128,1024]{1,0:T(8,128)(2,1)}) custom-call(s32[16]{0:T(128)S(1)} %get-tuple-element.109.seg_ref, s32[1]{0:T(128)} %bitcast.1.x_ref, bf16[4,128,1024]{2,1,0:T(8,128)(2,1)S(1)} %reshape.343.q_ref, ...), custom_call_target="tpu_custom_call" | custom-call | flops 65536 | bytes 65536 | tf_op jit(solution)/shard_map/pallas_call | solution.py:237
  244.0 3.4 %copy-done.3 = bf16[1024,4096]{1,0:T(8,128)(2,1)S(1)} copy-done((bf16[1024,4096]{1,0:T(8,128)(2,1)S(1)}, bf16[1024,4096]{1,0:T(8,128)(2,1)}, u32[]{:S(2)}) %copy-start.3) | copy-done | bytes 8388632
  249.5 2.9 %collective-permute-done.11.refs_1_ = bf16[128,1024]{1,0:T(8,128)(2,1)S(1)} collective-permute-done((bf16[128,1024]{1,0:T(8,128)(2,1)}, bf16[128,1024]{1,0:T(8,128)(2,1)S(1)}, u32[]{:S(2)}, u32[]{:S(2)}) %collective-permute-start.11) | collective-permute-done | bytes 262176 | tf_op jit(solution)/shard_map/ppermute | solution.py:313
  252.4 7.3 %shard_map.91.refs_0_ = f32[128,4096]{1,0:T(8,128)S(1)} custom-call(s32[1]{0:T(128)} %bitcast.c_ref, f32[128,4096]{1,0:T(8,128)S(1)} %shard_map.90.refs_0_, bf16[128,1024]{1,0:T(8,128)(2,1)S(1)} %collective-permute-done.11.refs_1_, bf16[128,1024]{1,0:T(8,128)(2,1)S(1)} %collective-permute-done.10.refs_2_, bf16[1024,4096]{1,0:T(8,128)(2,1)} %collective-permute-done.6.refs_3_, ...), custom_call_target="tpu_custom_call" | custom-call | flops 2147483648 | bytes 16777216 | tf_op jit(solution)/shard_map/pallas_call | solution.py:275
  259.8 5.1 %shard_map.92 = bf16[128,4096]{1,0:T(8,128)(2,1)} custom-call(s32[1]{0:T(128)} %bitcast.c_ref, f32[128,4096]{1,0:T(8,128)S(1)} %shard_map.91.refs_0_, bf16[128,1024]{1,0:T(8,128)(2,1)S(1)} %collective-permute-done.12.refs_1_, bf16[1024,4096]{1,0:T(8,128)(2,1)} %collective-permute-done.13.refs_2_), custom_call_target="tpu_custom_call" | custom-call | flops 1073741824 | bytes 8388608 | tf_op jit(solution)/shard_map/pallas_call | solution.py:275
  (134 shorter events, 48.0 us)
Async XLA Ops:
  0.0 8.3 %copy-start = (s32[2048]{0:T(1024)S(1)}, s32[2048]{0:T(1024)}, u32[]{:S(2)}) copy-start(s32[2048]{0:T(1024)} %param.14) | copy-start | bytes 24580
  0.0 15.2 %copy-start.17 = (bf16[512,1024]{1,0:T(8,128)(2,1)S(1)}, bf16[512,1024]{1,0:T(8,128)(2,1)}, u32[]{:S(2)}) copy-start(bf16[512,1024]{1,0:T(8,128)(2,1)} %param.8) | copy-start | bytes 3145732
  0.0 126.4 %collective-permute-start.6 = (bf16[1024,4096]{1,0:T(8,128)(2,1)}, bf16[1024,4096]{1,0:T(8,128)(2,1)}, u32[]{:S(2)}, u32[]{:S(2)}) collective-permute-start(bf16[1024,4096]{1,0:T(8,128)(2,1)} %refs_1_.1), channel_id=1, source_target_pairs={{0,3},{1,0},{2,1},{3,2},{4,5},{5,6},{6,7},{7,4},{8,11},{9,8},{10,9... | collective-permute-start | bytes 25165832 | tf_op jit(solution)/shard_map/ppermute | solution.py:334
  0.8 55.3 %collective-permute-start = (bf16[32,128,256]{2,1,0:T(8,128)(2,1)}, bf16[32,128,256]{2,1,0:T(8,128)(2,1)}, u32[]{:S(2)}, u32[]{:S(2)}) collective-permute-start(bf16[32,128,256]{2,1,0:T(8,128)(2,1)} %refs_0_.1), channel_id=1, source_target_pairs={{0,32},{4,36},{8,40},{12,44},{16,48},{20,52},{24,56},{28,60},{32,6... | collective-permute-start | bytes 6291464 | tf_op jit(solution)/shard_map/ppermute | solution.py:310
  2.8 53.4 %collective-permute-start.2 = (bf16[32,128,256]{2,1,0:T(8,128)(2,1)}, bf16[32,128,256]{2,1,0:T(8,128)(2,1)}, u32[]{:S(2)}, u32[]{:S(2)}) collective-permute-start(bf16[32,128,256]{2,1,0:T(8,128)(2,1)} %refs_0_.1), channel_id=1, source_target_pairs={{0,224},{4,228},{8,232},{12,236},{16,240},{20,244},{24,248},{28,25... | collective-permute-start | bytes 6291464 | tf_op jit(solution)/shard_map/ppermute | solution.py:310
  10.7 11.6 %all-to-all-start = ((s32[8,1,16]{2,1,0:T(1,128)}), s32[8,1,16]{2,1,0:T(1,128)S(1)}, u32[]{:S(2)}, u32[]{:S(2)}) async-start(s32[8,1,16]{2,1,0:T(1,128)} %copy.44), calls=%async_computation | async-start | bytes 8192 | tf_op jit(solution)/shard_map/all_to_all | solution.py:321
  17.2 5.5 %copy-start.18 = (bf16[16,256]{1,0:T(8,128)(2,1)S(1)}, bf16[16,256]{1,0:T(8,128)(2,1)}, u32[]{:S(2)}) copy-start(bf16[16,256]{1,0:T(8,128)(2,1)} %param.10) | copy-start | bytes 24580
  17.2 39.0 %copy-start.4 = (bf16[32,128,256]{2,1,0:T(8,128)(2,1)S(1)}, bf16[32,128,256]{2,1,0:T(8,128)(2,1)}, u32[]{:S(2)}) copy-start(bf16[32,128,256]{2,1,0:T(8,128)(2,1)} %refs_0_.1) | copy-start | bytes 6291460
  23.4 32.8 %all-to-all-start.1 = ((bf16[8,32,256]{2,1,0:T(8,128)(2,1)}), bf16[8,32,256]{2,1,0:T(8,128)(2,1)S(1)}, u32[]{:S(2)}, u32[]{:S(2)}) async-start(bf16[8,32,256]{2,1,0:T(8,128)(2,1)} %broadcast_in_dim.44), calls=%async_computation.1 | async-start | bytes 262144 | tf_op jit(solution)/shard_map/all_to_all | solution.py:376
  61.6 64.8 %all-to-all-start.2 = ((bf16[8,7,128,256]{3,2,1,0:T(8,128)(2,1)}), bf16[8,7,128,256]{3,2,1,0:T(8,128)(2,1)}, u32[]{:S(2)}, u32[]{:S(2)}) async-start(bf16[8,7,128,256]{3,2,1,0:T(8,128)(2,1)} %bitcast.43), calls=%async_computation.2 | async-start | bytes 7340032 | tf_op jit(solution)/shard_map/all_to_all | solution.py:321
  66.2 49.4 %collective-permute-start.1 = (bf16[32,128,256]{2,1,0:T(8,128)(2,1)}, bf16[32,128,256]{2,1,0:T(8,128)(2,1)S(1)}, u32[]{:S(2)}, u32[]{:S(2)}) collective-permute-start(bf16[32,128,256]{2,1,0:T(8,128)(2,1)} %collective-permute-done.refs_1_), channel_id=1, source_target_pairs={{0,32},{4,36},{8,40},{12,44},{16,48},{20,52},{24,56},{28,60},{32,6... | collective-permute-start | bytes 6291464 | tf_op jit(solution)/shard_map/ppermute | solution.py:310
  69.4 47.9 %collective-permute-start.3 = (bf16[32,128,256]{2,1,0:T(8,128)(2,1)}, bf16[32,128,256]{2,1,0:T(8,128)(2,1)}, u32[]{:S(2)}, u32[]{:S(2)}) collective-permute-start(bf16[32,128,256]{2,1,0:T(8,128)(2,1)} %collective-permute-done.2.refs_2_), channel_id=1, source_target_pairs={{0,224},{4,228},{8,232},{12,236},{16,240},{20,244},{24,248},{28,25... | collective-permute-start | bytes 6291464 | tf_op jit(solution)/shard_map/ppermute | solution.py:310
  126.4 105.9 %collective-permute-start.9 = (bf16[1024,4096]{1,0:T(8,128)(2,1)}, bf16[1024,4096]{1,0:T(8,128)(2,1)}, u32[]{:S(2)}, u32[]{:S(2)}) collective-permute-start(bf16[1024,4096]{1,0:T(8,128)(2,1)} %collective-permute-done.6.refs_3_), channel_id=1, source_target_pairs={{0,4},{4,0},{8,12},{12,8},{16,20},{20,16},{24,28},{28,24},{32,36},... | collective-permute-start | bytes 25165832 | tf_op jit(solution)/shard_map/ppermute | solution.py:316
  126.4 133.4 %collective-permute-start.13 = (bf16[1024,4096]{1,0:T(8,128)(2,1)}, bf16[1024,4096]{1,0:T(8,128)(2,1)}, u32[]{:S(2)}, u32[]{:S(2)}) collective-permute-start(bf16[1024,4096]{1,0:T(8,128)(2,1)} %collective-permute-done.6.refs_3_), channel_id=1, source_target_pairs={{0,3},{1,0},{2,1},{3,2},{4,5},{5,6},{6,7},{7,4},{8,11},{9,8},{10,9... | collective-permute-start | bytes 25165832 | tf_op jit(solution)/shard_map/ppermute | solution.py:334
  128.0 42.8 %all-to-all-start.3 = ((bf16[8,4,128,256]{3,2,1,0:T(8,128)(2,1)}), bf16[8,4,128,256]{3,2,1,0:T(8,128)(2,1)S(1)}, u32[]{:S(2)}, u32[]{:S(2)}) async-start(bf16[8,4,128,256]{3,2,1,0:T(8,128)(2,1)} %bitcast.45), calls=%async_computation.3 | async-start | bytes 4194304 | tf_op jit(solution)/shard_map/all_to_all | solution.py:321
  132.5 38.3 %collective-permute-start.4 = (bf16[12,2,128,256]{3,2,1,0:T(8,128)(2,1)}, bf16[12,2,128,256]{3,2,1,0:T(8,128)(2,1)}, u32[]{:S(2)}, u32[]{:S(2)}) collective-permute-start(bf16[12,2,128,256]{3,2,1,0:T(8,128)(2,1)} %bitcast.50), channel_id=1, source_target_pairs={{0,32},{4,36},{8,40},{12,44},{16,48},{20,52},{24,56},{28,60},{32,6... | collective-permute-start | bytes 4718600 | tf_op jit(solution)/shard_map/ppermute | solution.py:310
  133.0 37.8 %collective-permute-start.5 = (bf16[12,2,128,256]{3,2,1,0:T(8,128)(2,1)}, bf16[12,2,128,256]{3,2,1,0:T(8,128)(2,1)}, u32[]{:S(2)}, u32[]{:S(2)}) collective-permute-start(bf16[12,2,128,256]{3,2,1,0:T(8,128)(2,1)} %bitcast.49), channel_id=1, source_target_pairs={{0,224},{4,228},{8,232},{12,236},{16,240},{20,244},{24,248},{28,25... | collective-permute-start | bytes 4718600 | tf_op jit(solution)/shard_map/ppermute | solution.py:310
  176.2 31.8 %all-to-all-start.5 = ((bf16[8,4,128,256]{3,2,1,0:T(8,128)(2,1)}), bf16[8,4,128,256]{3,2,1,0:T(8,128)(2,1)}, u32[]{:S(2)}, u32[]{:S(2)}) async-start(bf16[8,4,128,256]{3,2,1,0:T(8,128)(2,1)} %bitcast.46), calls=%async_computation.5 | async-start | bytes 4194304 | tf_op jit(solution)/shard_map/all_to_all | solution.py:321
  180.6 15.8 %collective-permute-start.7 = (bf16[8,128,256]{2,1,0:T(8,128)(2,1)}, bf16[8,128,256]{2,1,0:T(8,128)(2,1)S(1)}, u32[]{:S(2)}, u32[]{:S(2)}) collective-permute-start(bf16[8,128,256]{2,1,0:T(8,128)(2,1)} %copy-done.15), channel_id=1, source_target_pairs={{0,32},{4,36},{8,40},{12,44},{16,48},{20,52},{24,56},{28,60},{32,6... | collective-permute-start | bytes 1572872 | tf_op jit(solution)/shard_map/ppermute | solution.py:310
  180.7 15.7 %collective-permute-start.8 = (bf16[8,128,256]{2,1,0:T(8,128)(2,1)}, bf16[8,128,256]{2,1,0:T(8,128)(2,1)S(1)}, u32[]{:S(2)}, u32[]{:S(2)}) collective-permute-start(bf16[8,128,256]{2,1,0:T(8,128)(2,1)} %copy-done.14), channel_id=1, source_target_pairs={{0,224},{4,228},{8,232},{12,236},{16,240},{20,244},{24,248},{28,25... | collective-permute-start | bytes 1572872 | tf_op jit(solution)/shard_map/ppermute | solution.py:310
  208.0 24.3 %all-to-all-start.4 = ((bf16[8,2,128,256]{3,2,1,0:T(8,128)(2,1)}), bf16[8,2,128,256]{3,2,1,0:T(8,128)(2,1)}, u32[]{:S(2)}, u32[]{:S(2)}) async-start(bf16[8,2,128,256]{3,2,1,0:T(8,128)(2,1)} %pad_maximum_fusion), calls=%async_computation.4 | async-start | bytes 2097152 | tf_op jit(solution)/shard_map/all_to_all | solution.py:321
  240.1 9.4 %collective-permute-start.10 = (bf16[128,1024]{1,0:T(8,128)(2,1)}, bf16[128,1024]{1,0:T(8,128)(2,1)S(1)}, u32[]{:S(2)}, u32[]{:S(2)}) collective-permute-start(bf16[128,1024]{1,0:T(8,128)(2,1)} %get-tuple-element.83), channel_id=1, source_target_pairs={{0,1},{1,2},{2,3},{3,0},{4,5},{5,6},{6,7},{7,4},{8,9},{9,10},{10,1... | collective-permute-start | bytes 786440 | tf_op jit(solution)/shard_map/ppermute | solution.py:313
  241.8 10.6 %collective-permute-start.11 = (bf16[128,1024]{1,0:T(8,128)(2,1)}, bf16[128,1024]{1,0:T(8,128)(2,1)S(1)}, u32[]{:S(2)}, u32[]{:S(2)}) collective-permute-start(bf16[128,1024]{1,0:T(8,128)(2,1)} %get-tuple-element.84), channel_id=1, source_target_pairs={{0,3},{1,0},{2,1},{3,2},{4,7},{5,4},{6,5},{7,6},{8,11},{9,8},{10,9... | collective-permute-start | bytes 786440 | tf_op jit(solution)/shard_map/ppermute | solution.py:313
  242.2 17.6 %collective-permute-start.12 = (bf16[128,1024]{1,0:T(8,128)(2,1)}, bf16[128,1024]{1,0:T(8,128)(2,1)S(1)}, u32[]{:S(2)}, u32[]{:S(2)}) collective-permute-start(bf16[128,1024]{1,0:T(8,128)(2,1)} %copy-done.16), channel_id=1, source_target_pairs={{0,2},{1,3},{2,0},{3,1},{4,6},{5,7},{6,4},{7,5},{8,10},{9,11},{10,... | collective-permute-start | bytes 786440 | tf_op jit(solution)/shard_map/ppermute | solution.py:313
  (15 other events, 26.8 us)
